TPU v7x, 512 devices: a whole 4x4x16 slice. The times are simulated.
512 devices in a mesh: orient: 128 (over z, x, core), dom: 4 (over y).
Axes of the slice: x: 4, y: 4, z: 16, core: 2. Of those that a mesh axis runs over, the one named last changes fastest.
Arguments:
- images: bfloat16 [1152, 2, 2048], P('dom'), may hold values from -9 to 9
- references: bfloat16 [4608, 2, 2048], P('orient'), may hold values from -3 to 3
- noise_weights: float32 [64, 2048], replicated, may hold values from 0.01 to 0.1
- log_prior: float32 [8, 16], replicated, may hold values from -6 to 6
- groups: int32 [1152], P('dom'), may hold values from 0 to 63
- prior_index: int32 [1152], P('dom'), may hold values from 0 to 7
- class_map: int32 [4608], P('orient'), may hold values from 0 to 15, as said below
Outputs:
- new_references: float32 [4608, 2, 2048], P('orient', None, 'dom')
- log_likelihood: float32 [1152], P('dom')
Inputs may be any that keep to these rules, and one draw needn't show every extreme that they name: `class_map`: each class owns one run of 288 consecutive orientations, a different class for each run.
All inputs are finite; a program needn't handle non-finite values.
Results may differ from a plain program's by a relative error of at most 0.0084.
Values sent between devices are 32-bit elements; how exact they have to be, the bound alone decides.
No kernel may reach another device: no remote copies, remote signals or barrier semaphores. Data moves between devices by JAX's collectives and lax.ppermute only.
A program may use at most 64 MiB of HBM per device.

v0:
```python
import jax
import jax.numpy as jnp
from jax import lax
from jax.sharding import PartitionSpec as P

BOX = 64
SHIFTS = 9


ridge = 0.01


def phase_tables(coeffs):
    coef_index = jnp.arange(coeffs, dtype=jnp.int32)
    row_id = coef_index // (BOX // 2)
    freq_y = (row_id + BOX // 2) % BOX - BOX // 2
    freq_x = coef_index % (BOX // 2)
    shift_id = jnp.arange(SHIFTS, dtype=jnp.int32)
    move_x = shift_id % 3 - 1
    move_y = shift_id // 3 - 1
    phase_angle = (move_x[:, None] * freq_x[None, :] + move_y[:, None] * freq_y[None, :]).astype(
        jnp.float32
    ) * (2.0 * jnp.pi / BOX)
    return (jnp.cos(phase_angle), jnp.sin(phase_angle))


def shift_references(ref_wide, phase_cos, phase_sin):
    real_part = (
        ref_wide[:, None, 0, :] * phase_cos[None] + ref_wide[:, None, 1, :] * phase_sin[None]
    )
    imag_part = (
        ref_wide[:, None, 1, :] * phase_cos[None] - ref_wide[:, None, 0, :] * phase_sin[None]
    )
    stacked = jnp.stack([real_part, imag_part], axis=2).astype(jnp.bfloat16)
    return stacked.reshape(ref_wide.shape[0] * SHIFTS, 2 * ref_wide.shape[2])


def rotate_back(products, phase_cos, phase_sin):
    real_sum = jnp.sum(
        products[:, :, 0] * phase_cos[None] - products[:, :, 1] * phase_sin[None], axis=1
    )
    imag_sum = jnp.sum(
        products[:, :, 0] * phase_sin[None] + products[:, :, 1] * phase_cos[None], axis=1
    )
    return jnp.stack([real_sum, imag_sum], axis=1)


def shards(images, references, noise_weights, log_prior, groups, prior_index, class_map):
    particle_rows = images.shape[0]
    orient_rows = references.shape[0]
    coeffs = images.shape[2]
    highest = lax.Precision.HIGHEST
    phase_cos, phase_sin = phase_tables(coeffs)
    group_hot = (
        groups[:, None] == jnp.arange(noise_weights.shape[0], dtype=jnp.int32)[None, :]
    ).astype(jnp.float32)
    weight_rows = jnp.dot(
        group_hot, noise_weights, precision=highest, preferred_element_type=jnp.float32
    )
    weighted = (images.astype(jnp.float32) * weight_rows[:, None, :]).astype(jnp.bfloat16)
    image_flat = weighted.reshape(particle_rows, 2 * coeffs)
    ref_wide = references.astype(jnp.float32)
    ref_power = ref_wide[:, 0] ** 2 + ref_wide[:, 1] ** 2
    quadratic = jnp.dot(
        noise_weights, ref_power.T, precision=highest, preferred_element_type=jnp.float32
    )
    shifted = shift_references(ref_wide, phase_cos, phase_sin)
    correlation = lax.dot_general(
        image_flat, shifted, (((1,), (1,)), ((), ())), preferred_element_type=jnp.float32
    )
    prior_hot = (
        prior_index[:, None] == jnp.arange(log_prior.shape[0], dtype=jnp.int32)[None, :]
    ).astype(jnp.float32)
    class_hot = (
        class_map[:, None] == jnp.arange(log_prior.shape[1], dtype=jnp.int32)[None, :]
    ).astype(jnp.float32)
    prior_table = jnp.dot(
        prior_hot, log_prior, precision=highest, preferred_element_type=jnp.float32
    )
    prior_rows = jnp.dot(
        prior_table, class_hot.T, precision=highest, preferred_element_type=jnp.float32
    )
    quad_rows = jnp.dot(group_hot, quadratic, precision=highest, preferred_element_type=jnp.float32)
    scores = (
        correlation.reshape(particle_rows, orient_rows, SHIFTS)
        + (prior_rows - 0.5 * quad_rows)[:, :, None]
    )
    local_peak = jnp.max(scores, axis=(1, 2))
    score_peak = lax.pmax(local_peak, "orient")
    score_mass = lax.psum(
        jnp.sum(jnp.exp(scores - score_peak[:, None, None]), axis=(1, 2)), "orient"
    )
    log_likelihood = score_peak + jnp.log(score_mass)
    posterior = jnp.exp(scores - log_likelihood[:, None, None]).astype(jnp.bfloat16)
    products = lax.dot_general(
        posterior.reshape(particle_rows, orient_rows * SHIFTS),
        image_flat,
        (((0,), (0,)), ((), ())),
        preferred_element_type=jnp.float32,
    )
    image_sums = rotate_back(products.reshape(orient_rows, SHIFTS, 2, coeffs), phase_cos, phase_sin)
    orient_mass = jnp.sum(posterior.astype(jnp.float32), axis=2)
    local_noise = lax.dot_general(
        orient_mass,
        weight_rows,
        (((0,), (0,)), ((), ())),
        precision=highest,
        preferred_element_type=jnp.float32,
    )
    summed_images, summed_noise = (
        lax.psum_scatter(image_sums, "dom", scatter_dimension=2, tiled=True),
        lax.psum_scatter(local_noise[:, None, :], "dom", scatter_dimension=2, tiled=True),
    )
    mass_share = summed_noise[:, 0, :]
    new_references = summed_images / (mass_share + ridge)[:, None, :]
    return (new_references, log_likelihood)


def solution(mesh):
    in_specs = (
        P("dom", None, None),
        P("orient", None, None),
        P(),
        P(),
        P("dom"),
        P("dom"),
        P("orient"),
    )
    out_specs = (P("orient", None, "dom"), P("dom"))
    return jax.shard_map(shards, mesh=mesh, in_specs=in_specs, out_specs=out_specs, check_vma=False)
```

profile of v0, /device:TPU:1, one launch (start us, length us, event | category | flops | bytes accessed | tf_op | source)
XLA Modules:
  0.0 590.3 jit_solution(8461985999402288237)
XLA Ops:
  7.2 0.0 copy-start
  7.2 0.0 reduce-scatter.5.cloned.1.call-start
  7.3 1.1 copy_convert_fusion
  8.5 0.6 fusion.18
  9.1 1.1 fusion.23
  10.2 0.3 convolution_multiply_fusion
  10.5 0.3 fusion.24
  10.8 5.5 multiply_convert_fusion
  16.3 0.2 convolution_subtract_fusion
  16.6 0.6 fusion.26
  17.2 0.8 add_convert_fusion
  17.9 0.1 copy-done.1
  18.0 2.6 fusion.42
  20.7 254.4 %pmax.7 = f32[288]{0:T(512)S(1)} all-reduce(f32[288]{0:T(512)S(1)} %get-tuple-element.16), channel_id=1, replica_groups=mesh['orient'=128,'dom'=4] {'orient'}, use_global_device_ids=true, to_apply=%region_1.2 | all-reduce | flops 288 | bytes 2304 | tf_op jit(solution)/shard_map/pmax | solution.py:89
  275.1 0.1 exponential_reduce_fusion
  275.2 251.2 %psum.7 = f32[288]{0:T(512)S(1)} all-reduce(f32[288]{0:T(512)S(1)} %exponential_reduce_fusion), channel_id=1, replica_groups=mesh['orient'=128,'dom'=4] {'orient'}, use_global_device_ids=true, to_apply=%region_3.4 | all-reduce | flops 288 | bytes 2304 | tf_op jit(solution)/shard_map/psum | solution.py:90
  526.4 0.8 convert_reduce_fusion
  527.2 2.3 convolution_bitcast_fusion
  529.5 0.0 reduce-scatter.5.cloned.1.call-update
  529.6 0.2 reduce-scatter.3.cloned.1.call-start
  529.8 0.1 copy.21
  529.9 0.2 reshape.212
  530.0 0.1 dot_general.39
  530.2 3.7 fusion.4
  534.0 0.9 subtract_reduce_fusion
  534.8 0.9 pad_maximum_fusion
  535.8 0.0 reduce-scatter.3.cloned.1.call-update
  535.8 12.8 %reduce-scatter.5.cloned.1.call-done = f32[36,1,512]{2,0,1:T(8,128)} async-done(((f32[36,1,2048]{2,0,1:T(8,128)}), f32[36,1,512]{2,0,1:T(8,128)}) %reduce-scatter.5.cloned.1.call-update) | async-done | bytes 73744 | tf_op jit(solution)/shard_map/reduce_scatter | solution.py:112
  548.6 0.9 add_bitcast_fusion
  549.5 32.2 %reduce-scatter.3.cloned.1.call-done = f32[36,2,512]{2,0,1:T(8,128)} async-done(((f32[36,2,2048]{2,0,1:T(8,128)}), f32[36,2,512]{2,0,1:T(8,128)}) %reduce-scatter.3.cloned.1.call-update) | async-done | bytes 147472 | tf_op jit(solution)/shard_map/reduce_scatter | solution.py:111
  581.7 0.9 broadcast_divide_fusion
  582.7 0.8 copy.25
  (26 shorter events, 0.1 us)
Async XLA Ops:
  7.2 1.3 copy-start
  7.2 1.9 copy-start.8
  7.2 541.4 %reduce-scatter.5.cloned.1.call-start = ((), (), s32[]{:S(2)}) async-start(), calls=%async_computation.3 | async-start | bytes 409600 | tf_op jit(solution)/shard_map/reduce_scatter | solution.py:112
  7.3 3.2 copy-start.10
  7.3 3.2 copy-start.11
  10.8 5.5 copy-start.9
  16.3 1.7 copy-start.1
  17.1 3.5 copy-start.2
  17.1 3.5 copy-start.4
  526.4 3.8 copy-start.7
  527.2 2.6 copy-start.6
  529.6 52.2 %reduce-scatter.3.cloned.1.call-start = ((), (), s32[]{:S(2)}) async-start(), calls=%async_computation.2 | async-start | bytes 819200 | tf_op jit(solution)/shard_map/reduce_scatter | solution.py:111
  530.2 3.8 copy-start.3
  530.2 3.8 copy-start.5
Sparse Core Ops, SparseCore 0:
  529.7 18.8 reduce-scatter.4
  551.4 30.2 reduce-scatter.2
where the time goes:
time: 591 us; the launch traced here: 590 us
  blocking collectives  506 us (86%)
  waiting for transfers between devices  45.1 us (8%)
  between operations  14.3 us (2%)
  other arithmetic  12.6 us (2%)
  matrix products  11.1 us (2%)
    pmax x1, blocking collectives, shards(): score_peak = lax.pmax(local_peak, 'orient')  254 us
    psum x1, blocking collectives, shards(): lax.psum(jnp.sum(jnp.exp(scores - score_peak[:, None, None]), axis=(1, 2)...  251 us
    reduce_scatter x1, waiting for transfers between devices, shards(): lax.psum_scatter(image_sums, 'dom', scatter_dimension=2, tiled=True)  32.2 us
    reduce_scatter x1, waiting for transfers between devices, shards(): lax.psum_scatter(local_noise[:, None, :], 'dom', scatter_dimension=2, til...  12.8 us
  transfers between devices with their start and end apart: 2, of which 2 were waited for; matrix products, arithmetic and copies ran while one was open for 1% of the time, Pallas kernels for 0%

commit v1 on v0

--- a/solution.py
+++ b/solution.py
@@ -1,6 +1,7 @@
 import jax
 import jax.numpy as jnp
 from jax import lax
+from jax.sharding import Mesh
 from jax.sharding import PartitionSpec as P
 
 BOX = 64
@@ -45,6 +46,16 @@
     return jnp.stack([real_sum, imag_sum], axis=1)
 
 
+def exchange(row, axes, count):
+    spread = jnp.broadcast_to(row[None, None, :], (count, 1, row.shape[0]))
+    return lax.all_to_all(spread, axes, 0, 0, tiled=True)[:, 0, :]
+
+
+def log_sum(rows):
+    peak = jnp.max(rows, axis=0)
+    return peak + jnp.log(jnp.sum(jnp.exp(rows - peak[None]), axis=0))
+
+
 def shards(images, references, noise_weights, log_prior, groups, prior_index, class_map):
     particle_rows = images.shape[0]
     orient_rows = references.shape[0]
@@ -86,11 +97,10 @@
         + (prior_rows - 0.5 * quad_rows)[:, :, None]
     )
     local_peak = jnp.max(scores, axis=(1, 2))
-    score_peak = lax.pmax(local_peak, "orient")
-    score_mass = lax.psum(
-        jnp.sum(jnp.exp(scores - score_peak[:, None, None]), axis=(1, 2)), "orient"
-    )
-    log_likelihood = score_peak + jnp.log(score_mass)
+    local_mass = jnp.sum(jnp.exp(scores - local_peak[:, None, None]), axis=(1, 2))
+    partial = local_peak + jnp.log(local_mass)
+    partial = log_sum(exchange(partial, "z", 16))
+    log_likelihood = log_sum(exchange(partial, ("x", "core"), 8))
     posterior = jnp.exp(scores - log_likelihood[:, None, None]).astype(jnp.bfloat16)
     products = lax.dot_general(
         posterior.reshape(particle_rows, orient_rows * SHIFTS),
@@ -100,31 +110,47 @@
     )
     image_sums = rotate_back(products.reshape(orient_rows, SHIFTS, 2, coeffs), phase_cos, phase_sin)
     orient_mass = jnp.sum(posterior.astype(jnp.float32), axis=2)
-    local_noise = lax.dot_general(
+    group_mass = lax.dot_general(
         orient_mass,
-        weight_rows,
+        group_hot,
         (((0,), (0,)), ((), ())),
         precision=highest,
         preferred_element_type=jnp.float32,
     )
-    summed_images, summed_noise = (
-        lax.psum_scatter(image_sums, "dom", scatter_dimension=2, tiled=True),
-        lax.psum_scatter(local_noise[:, None, :], "dom", scatter_dimension=2, tiled=True),
+    parts = 4
+    width = coeffs // parts
+    blocks = image_sums.reshape(2 * orient_rows, parts, width).transpose(1, 0, 2)
+    mass_rows = jnp.pad(group_mass.reshape(-1), (0, 8 * width - group_mass.size)).reshape(8, width)
+    blocks = jnp.concatenate(
+        [blocks, jnp.broadcast_to(mass_rows[None], (parts, 8, width))], axis=1
     )
-    mass_share = summed_noise[:, 0, :]
+    received = jnp.sum(lax.all_to_all(blocks, "dom", 0, 0, tiled=True), axis=0)
+    summed_images = received[: 2 * orient_rows].reshape(orient_rows, 2, width)
+    summed_mass = received[2 * orient_rows :].reshape(-1)[: group_mass.size]
+    my_weights = lax.dynamic_slice_in_dim(
+        noise_weights, lax.axis_index("dom") * width, width, axis=1
+    )
+    mass_share = jnp.dot(
+        summed_mass.reshape(group_mass.shape),
+        my_weights,
+        precision=highest,
+        preferred_element_type=jnp.float32,
+    )
     new_references = summed_images / (mass_share + ridge)[:, None, :]
     return (new_references, log_likelihood)
 
 
 def solution(mesh):
+    fine = Mesh(mesh.devices.reshape(16, 4, 2, 4), ("z", "x", "core", "dom"))
+    orient = ("z", "x", "core")
     in_specs = (
         P("dom", None, None),
-        P("orient", None, None),
+        P(orient, None, None),
         P(),
         P(),
         P("dom"),
         P("dom"),
-        P("orient"),
+        P(orient),
     )
-    out_specs = (P("orient", None, "dom"), P("dom"))
-    return jax.shard_map(shards, mesh=mesh, in_specs=in_specs, out_specs=out_specs, check_vma=False)
+    out_specs = (P(orient, None, "dom"), P("dom"))
+    return jax.shard_map(shards, mesh=fine, in_specs=in_specs, out_specs=out_specs, check_vma=False)

time: 591 us -> 76.6 us (0.13)
  blocking collectives: 506 us -> 37.8 us
  waiting for transfers between devices: 45.1 us -> 9.93 us
  between operations: 14.3 us -> 1.01 us
    pmax x1 -> x0, blocking collectives: 254 us -> none  [shards(): score_peak = lax.pmax(local_peak, 'orient')]
    psum x1 -> x0, blocking collectives: 251 us -> none  [shards(): lax.psum(jnp.sum(jnp.exp(scores - score_peak[:, None, None]), axis=(1, 2)...]
    reduce_scatter x2 -> x0, waiting for transfers between devices: 45.1 us -> none  [the longest x1 32.2 us: shards(): lax.psum_scatter(image_sums, 'dom', scatter_dimension=2, tiled=True)]
    all_to_all x0 -> x2, blocking collectives: none -> 37.8 us  [exchange(): return lax.all_to_all(spread, axes, 0, 0, tiled=True)[:, 0, :]]
    all_to_all x0 -> x1, waiting for transfers between devices: none -> 9.93 us  [shards(): received = jnp.sum(lax.all_to_all(blocks, 'dom', 0, 0, tiled=True), axis=0)]
  transfers between devices with their start and end apart: 2 -> 1, of which waited for: 2 -> 1; matrix products, arithmetic and copies ran while one was open for 1% -> 0% of each run, Pallas kernels for 0% -> 0%
where the time goes in v1:
time: 76.6 us; the launch traced here: 76.3 us
  blocking collectives  37.8 us (49%)
  other arithmetic  9.97 us (13%)
  waiting for transfers between devices  9.93 us (13%)
  matrix products  8.97 us (12%)
  local copies, waits for them, and re-layouts  4.45 us (6%)
  starting transfers between devices  4.19 us (5%)
  between operations  1.01 us (1%)
    all_to_all x2, blocking collectives, exchange(): return lax.all_to_all(spread, axes, 0, 0, tiled=True)[:, 0, :]  37.8 us
    all_to_all x1, waiting for transfers between devices, shards(): received = jnp.sum(lax.all_to_all(blocks, 'dom', 0, 0, tiled=True), axis=0)  9.93 us
    convert_element_type x1, other arithmetic, shards(): (images.astype(jnp.float32) * weight_rows[:, None, :]).astype(jnp.bfloat16)  4.82 us
    all_to_all x1, starting transfers between devices, shards(): received = jnp.sum(lax.all_to_all(blocks, 'dom', 0, 0, tiled=True), axis=0)  4.19 us
    dot_general x1, matrix products, shards(): lax.dot_general(image_flat, shifted, (((1,), (1,)), ((), ())), preferred_...  2.58 us
    dot_general x1, matrix products, shards(): jnp.dot(group_hot, noise_weights, precision=highest, preferred_element_ty...  2.54 us
    dot_general x1, matrix products, shards(): lax.dot_general(posterior.reshape(particle_rows, orient_rows * SHIFTS), i...  2.05 us
  transfers between devices with their start and end apart: 1, of which 1 were waited for; matrix products, arithmetic and copies ran while one was open for 0% of the time, Pallas kernels for 0%

profile of v1, /device:TPU:1, one launch (start us, length us, event | category | flops | bytes accessed | tf_op | source)
XLA Modules:
  0.0 76.3 jit_solution(8245434499824599712)
XLA Ops:
  0.7 1.1 %copy_convert_fusion = f32[36,2,2048]{2,0,1:T(8,128)S(1)} fusion(bf16[36,2,2048]{2,1,0:T(2,128)(2,1)} %param.8), kind=kLoop, calls=%fused_computation.28 | loop fusion | flops 147456 | bytes 884736 | tf_op jit(solution)/shard_map/convert_element_type | solution.py:73
  1.9 0.6 fusion.18
  2.4 2.5 %fusion.24 = f32[288,2048]{1,0:T(8,128)} fusion(f32[64,2048]{1,0:T(8,128)S(1)} %copy-done, s32[288]{0:T(512)S(1)} %copy-done.5), kind=kOutput, calls=%fused_computation.37 | convolution fusion | flops 453003264 | bytes 2884736 | tf_op jit(solution)/shard_map/dot_general | solution.py:68
  5.0 0.3 convolution_multiply_fusion
  5.3 4.8 %multiply_convert_fusion = bf16[288,2,2048]{2,1,0:T(2,128)(2,1)S(1)} fusion(bf16[288,2,2048]{2,1,0:T(2,128)(2,1)} %param.7, f32[288,2048]{1,0:T(8,128)} %fusion.24), kind=kLoop, calls=%fused_computation | loop fusion | flops 3538944 | bytes 7077888 | tf_op jit(solution)/shard_map/convert_element_type | solution.py:71
  10.1 0.3 fusion.25
  10.4 0.2 convolution_subtract_fusion
  10.7 0.6 fusion.28
  11.2 0.8 %add_convert_fusion = (bf16[36,9,1,2048]{3,0,2,1:T(8,128)(2,1)S(1)}, bf16[36,9,1,2048]{3,0,2,1:T(8,128)(2,1)S(1)}) fusion(f32[9,2048]{1,0:T(8,128)S(1)} %get-tuple-element.11, f32[36,2048]{1,0:T(8,128)S(1)} %get-tuple-element.9, f32[9,2048]{1,0:T(8,128)S(1)} %get-tuple-element.10, f32[36,2048]{1,0:T(8,128)S(1)} %get-tuple-element.8), kind=kLoop, calls=%fused_computation.10 | loop fusion | flops 5308416 | bytes 3391488 | tf_op jit(solution)/shard_map/convert
  12.0 2.6 %fusion.51 = (f32[288]{0:T(512)S(1)}, f32[288,36,9]{0,1,2:T(8,128)S(1)}) fusion(f32[288,36]{0,1:T(8,128)S(1)} %convolution_subtract_fusion, bf16[36,9,1,2048]{3,0,2,1:T(8,128)(2,1)S(1)} %get-tuple-element.7, bf16[36,9,1,2048]{3,0,2,1:T(8,128)(2,1)S(1)} %get-tuple-element.6, bf16[288,2,2048]{2,1,0:T(2,128)(2,1)S(1)} %multiply_convert_fusion), kind=kOutput, calls=%fused_computation.85 | convolution fusion | flops 769906688 | bytes 5429376 | tf_op jit(solution)/shard_map/dot_general | solution.py:79
  14.6 0.1 exponential_reduce_fusion
  14.8 27.0 %all_to_all.15 = f32[16,1,288]{2,1,0:T(1,128)S(1)} all-to-all(f32[16,1,288]{2,1,0:T(1,128)S(1)} %broadcast_in_dim.8), channel_id=1, replica_groups=mesh['z'=16,'x'=4,'core'=2,'dom'=4] {'z'}, dimensions={0} | all-to-all | bytes 36864 | tf_op jit(solution)/shard_map/all_to_all | solution.py:51
  41.8 10.8 %all_to_all.16 = f32[8,1,288]{2,1,0:T(1,128)S(1)} all-to-all(f32[8,1,288]{2,1,0:T(1,128)S(1)} %broadcast_in_dim.9), channel_id=1, replica_groups=mesh['z'=16,'x'=4,'core'=2,'dom'=4] {'x','core'}, dimensions={0} | all-to-all | bytes 18432 | tf_op jit(solution)/shard_map/all_to_all | solution.py:51
  52.8 0.1 convert_reduce_fusion
  52.9 0.9 %reshape.250 = bf16[288,324]{0,1:T(8,128)(2,1)} reshape(bf16[288,36,9]{0,2,1:T(8,128)(2,1)S(1)} %copy.36) | data formatting | bytes 373248 | tf_op jit(solution)/shard_map/reshape | solution.py:106
  53.8 1.1 %dot_general.42 = bf16[36,9,288]{2,1,0:T(8,128)(2,1)S(1)} reshape(bf16[324,288]{1,0:T(8,128)(2,1)} %bitcast.78) | data formatting | bytes 373248 | tf_op jit(solution)/shard_map/dot_general | solution.py:105
  54.9 2.0 %fusion.4 = f32[36,9,2,2048]{3,0,2,1:T(8,128)S(1)} fusion(bf16[36,9,288,1]{2,1,0,3:T(8,128)(2,1)S(1)} %bitcast.77, bf16[36,8,2,2048]{3,2,1,0:T(2,128)(2,1)S(1)} %bitcast.75), kind=kOutput, calls=%fused_computation.12 | convolution fusion | flops 764411904 | bytes 7854336 | tf_op jit(solution)/shard_map/dot_general | solution.py:105
  57.0 0.9 %subtract_reduce_fusion = (f32[36,2048]{1,0:T(8,128)S(1)}, f32[36,2048]{1,0:T(8,128)S(1)}) fusion(f32[36,9,2,2048]{3,0,2,1:T(8,128)S(1)} %fusion.4, f32[9,2048]{1,0:T(8,128)S(1)} %copy-done.4, f32[9,2048]{1,0:T(8,128)S(1)} %copy-done.2), kind=kLoop, calls=%fused_computation.8 | loop fusion | flops 5160960 | bytes 6045696 | tf_op jit(solution)/shard_map/reduce_sum | solution.py:40
  57.8 0.2 stack.16
  58.0 0.2 stack.17
  58.3 0.5 pad_maximum_fusion.1
  58.8 0.6 reshape.252
  59.4 0.3 fusion.23
  59.7 0.1 reshape.253
  59.8 0.1 pad_maximum_fusion
  59.9 1.0 %copy.40 = f32[4,80,512]{2,1,0:T(8,128)} copy(f32[4,80,512]{2,0,1:T(4,128)S(1)} %pad_maximum_fusion) | data formatting | bytes 1310720 | tf_op jit(solution)/shard_map/concatenate | solution.py:124
  61.0 4.2 %all-to-all-start.2 = ((f32[4,80,512]{2,1,0:T(8,128)}), f32[4,80,512]{2,1,0:T(8,128)S(1)}, u32[]{:S(2)}, u32[]{:S(2)}) async-start(f32[4,80,512]{2,1,0:T(8,128)} %copy.40), calls=%async_computation.2 | async-start | bytes 1310720 | tf_op jit(solution)/shard_map/all_to_all | solution.py:127
  65.2 9.9 %all-to-all-done.2 = f32[4,80,512]{2,1,0:T(8,128)S(1)} async-done(((f32[4,80,512]{2,1,0:T(8,128)}), f32[4,80,512]{2,1,0:T(8,128)S(1)}, u32[]{:S(2)}, u32[]{:S(2)}) %all-to-all-start.2) | async-done | bytes 655392 | tf_op jit(solution)/shard_map/all_to_all | solution.py:127
  75.2 0.1 reshape.254
  75.3 0.1 slice.36
  75.3 0.2 convolution_add_fusion
  75.6 0.7 broadcast_divide_fusion
  (39 shorter events, 0.4 us)
Async XLA Ops:
  0.6 1.2 %copy-start = (f32[64,2048]{1,0:T(8,128)S(1)}, f32[64,2048]{1,0:T(8,128)}, u32[]{:S(2)}) copy-start(f32[64,2048]{1,0:T(8,128)} %param.9) | copy-start | bytes 1572868
  0.6 1.8 %copy-start.5 = (s32[288]{0:T(512)S(1)}, s32[288]{0:T(512)}, u32[]{:S(2)}) copy-start(s32[288]{0:T(512)} %param.11) | copy-start | bytes 3460
  5.3 4.9 %copy-start.8 = (f32[8,16]{1,0:T(8,128)S(1)}, f32[8,16]{1,0:T(8,128)}, u32[]{:S(2)}) copy-start(f32[8,16]{1,0:T(8,128)} %param.10) | copy-start | bytes 1540
  5.3 4.9 %copy-start.9 = (s32[288]{0:T(512)S(1)}, s32[288]{0:T(512)}, u32[]{:S(2)}) copy-start(s32[288]{0:T(512)} %param.12) | copy-start | bytes 3460
  5.3 5.1 %copy-start.7 = (s32[36]{0:T(128)S(1)}, s32[36]{0:T(128)}, u32[]{:S(2)}) copy-start(s32[36]{0:T(128)} %param.13) | copy-start | bytes 436
  11.2 3.4 %copy-start.1 = (f32[9,2048]{1,0:T(8,128)}, f32[9,2048]{1,0:T(8,128)S(1)}, u32[]{:S(2)}) copy-start(f32[9,2048]{1,0:T(8,128)S(1)} %get-tuple-element.10) | copy-start | bytes 221188
  11.2 3.4 %copy-start.3 = (f32[9,2048]{1,0:T(8,128)}, f32[9,2048]{1,0:T(8,128)S(1)}, u32[]{:S(2)}) copy-start(f32[9,2048]{1,0:T(8,128)S(1)} %get-tuple-element.11) | copy-start | bytes 221188
  52.7 4.2 %copy-start.6 = (f32[288]{0:T(512)}, f32[288]{0:T(512)S(1)}, u32[]{:S(2)}) copy-start(f32[288]{0:T(512)S(1)} %log_add_fusion) | copy-start | bytes 3460
  54.9 2.1 %copy-start.2 = (f32[9,2048]{1,0:T(8,128)S(1)}, f32[9,2048]{1,0:T(8,128)}, u32[]{:S(2)}) copy-start(f32[9,2048]{1,0:T(8,128)} %copy-done.1) | copy-start | bytes 221188
  54.9 2.1 %copy-start.4 = (f32[9,2048]{1,0:T(8,128)S(1)}, f32[9,2048]{1,0:T(8,128)}, u32[]{:S(2)}) copy-start(f32[9,2048]{1,0:T(8,128)} %copy-done.3) | copy-start | bytes 221188
  61.0 14.1 %all-to-all-start.2 = ((f32[4,80,512]{2,1,0:T(8,128)}), f32[4,80,512]{2,1,0:T(8,128)S(1)}, u32[]{:S(2)}, u32[]{:S(2)}) async-start(f32[4,80,512]{2,1,0:T(8,128)} %copy.40), calls=%async_computation.2 | async-start | bytes 1310720 | tf_op jit(solution)/shard_map/all_to_all | solution.py:127

commit v2 on v0

v2 whole, which is shorter than its diff:
```python
import functools

import jax
import jax.numpy as jnp
import numpy as np
from jax import lax
from jax.experimental import pallas as pl
from jax.experimental.pallas import tpu as pltpu
from jax.sharding import Mesh
from jax.sharding import PartitionSpec as P

BOX = 64
RIDGE = 0.01
LANES = 128
PAIRS = (5, 6, 7, 8)
LOWEST = -1.0e30
HIGHEST = lax.Precision.HIGHEST
VMEM_BYTES = 50 * 1024 * 1024


def phase_tables(coeffs):
    index = np.arange(coeffs)
    row = index // (BOX // 2)
    freq_y = (row + BOX // 2) % BOX - BOX // 2
    freq_x = index % (BOX // 2)
    shift = np.array(PAIRS)
    turns = (shift % 3 - 1)[:, None] * freq_x[None] + (shift // 3 - 1)[:, None] * freq_y[None]
    angle = (turns % BOX) * (2.0 * np.pi / BOX)
    return np.concatenate([np.cos(angle), np.sin(angle)]).astype(np.float32)


def split_bf16(values):
    high = values.astype(jnp.bfloat16)
    rest = values - high.astype(jnp.float32)
    mid = rest.astype(jnp.bfloat16)
    low = (rest - mid.astype(jnp.float32)).astype(jnp.bfloat16)
    return high, mid, low


def log_sum(rows):
    peak = jnp.max(rows, axis=0, keepdims=True)
    return peak + jnp.log(jnp.sum(jnp.exp(rows - peak), axis=0, keepdims=True))


def hot_columns(count, index_row):
    rows = lax.broadcasted_iota(jnp.int32, (count, index_row.shape[1]), 0)
    return rows == index_row


def score_kernel(
    images_ref,
    refs_ref,
    noise_ref,
    prior_ref,
    groups_ref,
    prior_index_ref,
    class_ref,
    phase_ref,
    scores_ref,
    weighted_ref,
    partial_ref,
    images_vmem,
    image_wide,
    ref_wide,
    shifted,
    weights,
    power,
    image_sem,
):
    particles = groups_ref.shape[1]
    coeffs = noise_ref.shape[1]
    ngroups = noise_ref.shape[0]
    blocks = coeffs // LANES
    orients = class_ref.shape[0]
    padded = (orients + 7) // 8 * 8
    stride = 2 * blocks
    fetch = pltpu.make_async_copy(images_ref, images_vmem, image_sem)
    fetch.start()

    ref_wide[0 : orients * stride, :] = refs_ref[...].astype(jnp.float32)
    ref_wide[orients * stride :, :] = jnp.zeros(
        ((padded - orients) * stride, LANES), jnp.float32
    )
    group_hot = hot_columns(ngroups, groups_ref[...])
    group_bf16 = group_hot.astype(jnp.float32).astype(jnp.bfloat16)
    noise_parts = jnp.concatenate(split_bf16(noise_ref[...]), axis=0)
    weights[...] = lax.dot_general(
        jnp.concatenate([group_bf16] * 3, axis=0),
        noise_parts,
        (((0,), (0,)), ((), ())),
        preferred_element_type=jnp.float32,
    )

    @pl.loop(0, blocks)
    def _(b):
        here = pl.ds(pl.multiple_of(b * LANES, LANES), LANES)
        real = ref_wide[pl.ds(2 * b, padded, stride=stride), :]
        imag = ref_wide[pl.ds(2 * b + 1, padded, stride=stride), :]
        power[:, here] = real * real + imag * imag
        reals = [real, jnp.zeros((8, LANES), jnp.float32)]
        imags = [imag, jnp.zeros((8, LANES), jnp.float32)]
        for k in range(4):
            cosine = phase_ref[k : k + 1, here]
            sine = phase_ref[k + 4 : k + 5, here]
            real_cos, real_sin = real * cosine, real * sine
            imag_cos, imag_sin = imag * cosine, imag * sine
            reals += [real_cos + imag_sin, real_cos - imag_sin]
            imags += [imag_cos - real_sin, imag_cos + real_sin]
        wide = pl.multiple_of(b * 2 * LANES, 2 * LANES)
        shifted[:, pl.ds(wide, LANES)] = jnp.concatenate(reals, axis=0).astype(jnp.bfloat16)
        shifted[:, pl.ds(wide + LANES, LANES)] = jnp.concatenate(imags, axis=0).astype(
            jnp.bfloat16
        )

    quadratic = lax.dot_general(
        power[...],
        noise_ref[...],
        (((1,), (1,)), ((), ())),
        precision=HIGHEST,
        preferred_element_type=jnp.float32,
    )
    classes = prior_ref.shape[1]
    class_hot = (
        lax.broadcasted_iota(jnp.int32, (orients, classes), 1) == class_ref[...]
    ).astype(jnp.float32)
    class_hot = jnp.concatenate(
        [class_hot, jnp.zeros((padded - orients, classes), jnp.float32)], axis=0
    )
    class_prior = lax.dot_general(
        class_hot,
        prior_ref[...],
        (((1,), (1,)), ((), ())),
        precision=HIGHEST,
        preferred_element_type=jnp.float32,
    )
    prior_hot = hot_columns(prior_ref.shape[0], prior_index_ref[...]).astype(jnp.float32)
    offsets = jnp.dot(
        class_prior, prior_hot, precision=HIGHEST, preferred_element_type=jnp.float32
    ) - 0.5 * jnp.dot(
        quadratic,
        group_hot.astype(jnp.float32),
        precision=HIGHEST,
        preferred_element_type=jnp.float32,
    )
    real_row = lax.broadcasted_iota(jnp.int32, (padded, particles), 0) < orients
    offsets = jnp.where(real_row, offsets, LOWEST)

    fetch.wait()

    @pl.loop(0, blocks)
    def _(b):
        part = particles // blocks * stride
        rows = pl.ds(pl.multiple_of(b * part, part), part)
        image_wide[rows, :] = images_vmem[rows, :].astype(jnp.float32)

    @pl.loop(0, blocks)
    def _(b):
        here = pl.ds(pl.multiple_of(b * LANES, LANES), LANES)
        weight = weights[:, here]
        wide = pl.multiple_of(b * 2 * LANES, 2 * LANES)
        for part in range(2):
            picked = image_wide[pl.ds(2 * b + part, particles, stride=stride), :]
            weighted_ref[:, pl.ds(wide + part * LANES, LANES)] = (picked * weight).astype(
                jnp.bfloat16
            )

    correlation = lax.dot_general(
        shifted[...],
        weighted_ref[...],
        (((1,), (1,)), ((), ())),
        preferred_element_type=jnp.float32,
    )
    scores = correlation + jnp.concatenate(
        [offsets, jnp.full((8, particles), LOWEST, jnp.float32)] + [offsets] * 8, axis=0
    )
    scores_ref[...] = scores
    partial_ref[...] = jnp.broadcast_to(log_sum(scores)[None], partial_ref.shape)


def update_kernel(
    partial_ref, scores_ref, weighted_ref, groups_ref, phase_ref, ngroups, likelihood_ref, out_ref
):
    orients = (out_ref.shape[1] - 8) // 2
    padded = (orients + 7) // 8 * 8
    width = out_ref.shape[2]
    likelihood = log_sum(partial_ref[:, 0, :])
    likelihood_ref[...] = likelihood
    posterior = jnp.exp(scores_ref[...] - likelihood).astype(jnp.bfloat16)
    group_hot = hot_columns(ngroups, groups_ref[...]).astype(jnp.float32).astype(jnp.bfloat16)
    mass = lax.dot_general(
        posterior, group_hot, (((1,), (1,)), ((), ())), preferred_element_type=jnp.float32
    )
    group_mass = mass[0:padded]
    for k in range(8):
        group_mass += mass[48 + k * padded : 48 + (k + 1) * padded]
    pieces = [group_mass[r : r + 8] for r in range(0, padded, 8)]
    room = width - ngroups * len(pieces)
    mass_rows = jnp.concatenate(pieces + [jnp.zeros((8, room), jnp.float32)], axis=1)
    for share in range(out_ref.shape[0]):
        out_ref[share, 2 * orients :, :] = mass_rows
        for step in range(width // LANES):
            b = share * (width // LANES) + step
            here = slice(b * LANES, (b + 1) * LANES)
            product = jnp.dot(
                posterior,
                weighted_ref[:, 2 * b * LANES : 2 * (b + 1) * LANES],
                preferred_element_type=jnp.float32,
            )
            real = product[0:padded, 0:LANES]
            imag = product[0:padded, LANES:]
            for k in range(4):
                cosine = phase_ref[k : k + 1, here]
                sine = phase_ref[k + 4 : k + 5, here]
                low = 48 + 2 * padded * k
                ahead = product[low : low + padded]
                behind = product[low + padded : low + 2 * padded]
                both, apart = ahead + behind, ahead - behind
                real += both[:, 0:LANES] * cosine - apart[:, LANES:] * sine
                imag += apart[:, 0:LANES] * sine + both[:, LANES:] * cosine
            there = slice(step * LANES, (step + 1) * LANES)
            out_ref[share, 0:orients, there] = real[0:orients]
            out_ref[share, orients : 2 * orients, there] = imag[0:orients]


def divide_kernel(share_ref, received_ref, noise_ref, out_ref):
    del share_ref
    rows = received_ref.shape[1]
    width = received_ref.shape[2]
    orients = (rows - 8) // 2
    padded = (orients + 7) // 8 * 8
    ngroups = noise_ref.shape[0]
    total = received_ref[0]
    for peer in range(1, received_ref.shape[0]):
        total += received_ref[peer]
    packed = total[2 * orients :]
    group_mass = jnp.concatenate(
        [packed[:, r * ngroups : (r + 1) * ngroups] for r in range(padded // 8)], axis=0
    )
    noise_mass = jnp.dot(
        group_mass, noise_ref[...], precision=HIGHEST, preferred_element_type=jnp.float32
    )
    scale = 1.0 / (noise_mass[0:orients] + RIDGE)
    for part in range(2):
        values = total[part * orients : (part + 1) * orients] * scale
        for b in range(width // LANES):
            out_ref[pl.ds(2 * b + part, orients, stride=2 * (width // LANES)), :] = values[
                :, b * LANES : (b + 1) * LANES
            ]


def rows_of(array):
    count, parts, coeffs = array.shape
    blocks = coeffs // LANES
    return (
        array.reshape(count, parts, blocks, LANES)
        .transpose(0, 2, 1, 3)
        .reshape(count * blocks * parts, LANES)
    )


def kernel_params():
    return pltpu.CompilerParams(vmem_limit_bytes=VMEM_BYTES)


def score_call(images, references, noise_weights, log_prior, groups, prior_index, class_map, phase, spread):
    particles, _, coeffs = images.shape
    orients = references.shape[0]
    padded = (orients + 7) // 8 * 8
    rows = 9 * padded + 8
    whole = pl.BlockSpec(memory_space=pltpu.VMEM)
    return pl.pallas_call(
        score_kernel,
        in_specs=[pl.BlockSpec(memory_space=pl.ANY)] + [whole] * 7,
        out_specs=[whole] * 3,
        out_shape=[
            jax.ShapeDtypeStruct((rows, particles), jnp.float32),
            jax.ShapeDtypeStruct((particles, 2 * coeffs), jnp.bfloat16),
            jax.ShapeDtypeStruct((spread, 1, particles), jnp.float32),
        ],
        scratch_shapes=[
            pltpu.VMEM((particles * 2 * coeffs // LANES, LANES), jnp.bfloat16),
            pltpu.VMEM((particles * 2 * coeffs // LANES, LANES), jnp.float32),
            pltpu.VMEM((padded * 2 * coeffs // LANES, LANES), jnp.float32),
            pltpu.VMEM((rows, 2 * coeffs), jnp.bfloat16),
            pltpu.VMEM((particles, coeffs), jnp.float32),
            pltpu.VMEM((padded, coeffs), jnp.float32),
            pltpu.SemaphoreType.DMA,
        ],
        compiler_params=kernel_params(),
        name="score",
    )(
        rows_of(images),
        rows_of(references),
        noise_weights,
        log_prior,
        groups[None, :],
        prior_index[None, :],
        class_map[:, None],
        phase,
    )


def update_call(partials, scores, weighted, groups, phase, ngroups, orients, shares):
    particles, wide = weighted.shape
    whole = pl.BlockSpec(memory_space=pltpu.VMEM)

    def body(partial_ref, scores_ref, weighted_ref, groups_ref, phase_ref, likelihood_ref, out_ref):
        update_kernel(
            partial_ref, scores_ref, weighted_ref, groups_ref, phase_ref, ngroups, likelihood_ref, out_ref
        )

    return pl.pallas_call(
        body,
        in_specs=[whole] * 5,
        out_specs=[whole] * 2,
        out_shape=[
            jax.ShapeDtypeStruct((1, particles), jnp.float32),
            jax.ShapeDtypeStruct((shares, 2 * orients + 8, wide // 2 // shares), jnp.float32),
        ],
        compiler_params=kernel_params(),
        name="update",
    )(partials, scores, weighted, groups[None, :], phase)


def divide_call(share, received, noise_weights):
    shares, rows, width = received.shape
    orients = (rows - 8) // 2
    ngroups = noise_weights.shape[0]
    return pl.pallas_call(
        divide_kernel,
        grid_spec=pltpu.PrefetchScalarGridSpec(
            num_scalar_prefetch=1,
            grid=(1,),
            in_specs=[
                pl.BlockSpec((shares, rows, width), lambda i, s: (0, 0, 0)),
                pl.BlockSpec((ngroups, width), lambda i, s: (0, s[0])),
            ],
            out_specs=pl.BlockSpec((orients * 2 * width // LANES, LANES), lambda i, s: (0, 0)),
        ),
        out_shape=jax.ShapeDtypeStruct((orients * 2 * width // LANES, LANES), jnp.float32),
        compiler_params=kernel_params(),
        name="divide",
    )(share, received, noise_weights)


def exchange(spread, axes):
    return lax.all_to_all(spread, axes, 0, 0, tiled=True)


def shards(images, references, noise_weights, log_prior, groups, prior_index, class_map):
    coeffs = images.shape[2]
    orients = references.shape[0]
    phase = jnp.asarray(phase_tables(coeffs))
    depth = lax.axis_size("z")
    plane = lax.axis_size("x") * lax.axis_size("core")
    shares = lax.axis_size("dom")
    scores, weighted, partial = score_call(
        images, references, noise_weights, log_prior, groups, prior_index, class_map, phase, depth
    )
    partial = log_sum(exchange(partial, "z")[:, 0, :])
    partial = jnp.broadcast_to(partial[None], (plane, 1, partial.shape[1]))
    partials = exchange(partial, ("x", "core"))
    likelihood, blocks = update_call(
        partials, scores, weighted, groups, phase, noise_weights.shape[0], orients, shares
    )
    received = exchange(blocks, "dom")
    share = lax.axis_index("dom").astype(jnp.int32)[None]
    new_rows = divide_call(share, received, noise_weights)
    width = coeffs // shares
    new_references = (
        new_rows.reshape(orients, width // LANES, 2, LANES)
        .transpose(0, 2, 1, 3)
        .reshape(orients, 2, width)
    )
    return (new_references, likelihood[0])


def solution(mesh):
    fine = Mesh(mesh.devices.reshape(16, 4, 2, 4), ("z", "x", "core", "dom"))
    orient = ("z", "x", "core")
    in_specs = (
        P("dom", None, None),
        P(orient, None, None),
        P(),
        P(),
        P("dom"),
        P("dom"),
        P(orient),
    )
    out_specs = (P(orient, None, "dom"), P("dom"))
    return jax.shard_map(shards, mesh=fine, in_specs=in_specs, out_specs=out_specs, check_vma=False)
```

time: 591 us -> 72.6 us (0.12)
  blocking collectives: 506 us -> 37.9 us
  waiting for transfers between devices: 45.1 us -> 9.33 us
  Pallas kernels: 0 us -> 13.7 us
  between operations: 14.3 us -> 0.67 us
  other arithmetic: 12.6 us -> 0.67 us
  matrix products: 11.1 us -> 0 us
    pmax x1 -> x0, blocking collectives: 254 us -> none  [shards(): score_peak = lax.pmax(local_peak, 'orient')]
    psum x1 -> x0, blocking collectives: 251 us -> none  [shards(): lax.psum(jnp.sum(jnp.exp(scores - score_peak[:, None, None]), axis=(1, 2)...]
    reduce_scatter x2 -> x0, waiting for transfers between devices: 45.1 us -> none  [the longest x1 32.2 us: shards(): lax.psum_scatter(image_sums, 'dom', scatter_dimension=2, tiled=True)]
    all_to_all x0 -> x2, blocking collectives: none -> 37.9 us  [exchange(): return lax.all_to_all(spread, axes, 0, 0, tiled=True)]
    pallas_call x0 -> x3, Pallas kernels: none -> 13.7 us  [the longest x1 10 us: score_call(): pl.pallas_call(score_kernel, in_specs=[pl.BlockSpec(memory_space=pl.ANY)]...]
    dot_general x8 -> x0, matrix products: 11.1 us -> none  [the longest x1 3.74 us: shards(): lax.dot_general(posterior.reshape(particle_rows, orient_rows * SHIFTS), i...]
    all_to_all x0 -> x1, waiting for transfers between devices: none -> 9.33 us  [exchange(): return lax.all_to_all(spread, axes, 0, 0, tiled=True)]
    convert_element_type x2 -> x0, other arithmetic: 6.68 us -> none  [the longest x1 5.53 us: shards(): (images.astype(jnp.float32) * weight_rows[:, None, :]).astype(jnp.bfloat16)]
  transfers between devices with their start and end apart: 2 -> 1, of which waited for: 2 -> 1; matrix products, arithmetic and copies ran while one was open for 1% -> 1% of each run, Pallas kernels for 0% -> 0%
where the time goes in v2:
time: 72.6 us; the launch traced here: 72.2 us
  blocking collectives  37.9 us (52%)
  Pallas kernels  13.7 us (19%)
  waiting for transfers between devices  9.33 us (13%)
  local copies, waits for them, and re-layouts  5.66 us (8%)
  starting transfers between devices  4.17 us (6%)
    all_to_all x2, blocking collectives, exchange(): return lax.all_to_all(spread, axes, 0, 0, tiled=True)  37.9 us
    pallas_call x1, Pallas kernels, score_call(): pl.pallas_call(score_kernel, in_specs=[pl.BlockSpec(memory_space=pl.ANY)]...  10 us
    all_to_all x1, waiting for transfers between devices, exchange(): return lax.all_to_all(spread, axes, 0, 0, tiled=True)  9.33 us
    all_to_all x1, starting transfers between devices, exchange(): return lax.all_to_all(spread, axes, 0, 0, tiled=True)  4.17 us
    unnamed x12, local copies, waits for them, and re-layouts  3.54 us
    pallas_call x1, Pallas kernels, update_call(): pl.pallas_call(body, in_specs=[whole] * 5, out_specs=[whole] * 2, out_sha...  2.74 us
  transfers between devices with their start and end apart: 1, of which 1 were waited for; matrix products, arithmetic and copies ran while one was open for 1% of the time, Pallas kernels for 0%

profile of v2, /device:TPU:1, one launch (start us, length us, event | category | flops | bytes accessed | tf_op | source)
XLA Modules:
  0.0 72.2 jit_solution(6723873328869003616)
XLA Ops:
  0.6 0.7 broadcast_in_dim.22.groups_ref
  1.3 0.7 %copy.12.class_ref = s32[36,1]{1,0:T(8,128)S(1)} copy(s32[36,1]{0,1:T(1,128)} %bitcast.26) | data formatting | bytes 288 | tf_op jit(solution)/shard_map/broadcast_in_dim | solution.py:298
  2.1 0.7 broadcast_in_dim.23.prior_index_ref
  2.7 0.0 copy-start
  2.7 1.0 %copy-done = f32[64,2048]{1,0:T(8,128)S(1)} copy-done((f32[64,2048]{1,0:T(8,128)S(1)}, f32[64,2048]{1,0:T(8,128)}, u32[]{:S(2)}) %copy-start) | copy-done | bytes 524312
  3.8 0.0 copy-start.2
  3.8 1.0 %copy-done.2 = bf16[36,2,2048]{2,1,0:T(2,128)(2,1)S(1)} copy-done((bf16[36,2,2048]{2,1,0:T(2,128)(2,1)S(1)}, bf16[36,2,2048]{2,1,0:T(2,128)(2,1)}, u32[]{:S(2)}) %copy-start.2) | copy-done | bytes 294936
  4.8 0.0 copy-start.3
  4.8 0.8 %copy-done.3 = f32[8,2048]{1,0:T(8,128)S(1)} copy-done((f32[8,2048]{1,0:T(8,128)S(1)}, f32[8,2048]{1,0:T(8,128)}, u32[]{:S(2)}) %copy-start.3) | copy-done | bytes 65560
  5.6 0.0 copy-start.5
  5.6 0.7 copy-done.5
  6.3 0.0 copy-start.4
  6.3 10.0 %score.1 = (f32[368,288]{1,0:T(8,128)S(1)}, bf16[288,4096]{1,0:T(8,128)(2,1)S(1)}, f32[16,1,288]{2,1,0:T(1,128)S(1)}) custom-call(bf16[9216,128]{1,0:T(8,128)(2,1)} %bitcast.24, bf16[1152,128]{1,0:T(8,128)(2,1)S(1)} %bitcast.23, f32[64,2048]{1,0:T(8,128)S(1)} %copy-done, f32[8,16]{1,0:T(8,128)S(1)} %copy-done.5, s32[1,288]{1,0:T(1,128)S(1)} %broadcast_in_dim.22.groups_ref, ...), custom_call_target="tpu_custom_call" | custom-call | tf_op jit(solution)/shard_map/score/pallas_call | solution.py:271
  16.3 0.0 copy-start.1
  16.3 27.1 %all_to_all.15 = f32[16,1,288]{2,1,0:T(1,128)S(1)} all-to-all(f32[16,1,288]{2,1,0:T(1,128)S(1)} %get-tuple-element.7), channel_id=1, replica_groups=mesh['z'=16,'x'=4,'core'=2,'dom'=4] {'z'}, dimensions={0} | all-to-all | bytes 36864 | tf_op jit(solution)/shard_map/all_to_all | solution.py:347
  43.5 10.8 %all_to_all.16.partial_ref = f32[8,1,288]{2,1,0:T(1,128)S(1)} all-to-all(f32[8,1,288]{2,1,0:T(1,128)S(1)} %broadcast_in_dim.25), channel_id=1, replica_groups=mesh['z'=16,'x'=4,'core'=2,'dom'=4] {'x','core'}, dimensions={0} | all-to-all | bytes 18432 | tf_op jit(solution)/shard_map/all_to_all | solution.py:347
  54.4 0.0 copy-done.4
  54.4 2.7 %update.1 = (f32[1,288]{1,0:T(1,128)S(1)}, f32[4,80,512]{2,1,0:T(8,128)}) custom-call(f32[8,1,288]{2,1,0:T(1,128)S(1)} %all_to_all.16.partial_ref, f32[368,288]{1,0:T(8,128)S(1)} %get-tuple-element.8.scores_ref, bf16[288,4096]{1,0:T(8,128)(2,1)S(1)} %get-tuple-element.9.weighted_ref, s32[1,288]{1,0:T(1,128)S(1)} %broadcast_in_dim.22.groups_ref, ...), custom_call_target="tpu_custom_call" | custom-call | tf_op jit(solution)/shard_map/update/pallas_call | solution.py:312
  57.1 4.2 %all-to-all-start.2 = ((f32[4,80,512]{2,1,0:T(8,128)}), f32[4,80,512]{2,1,0:T(8,128)S(1)}, u32[]{:S(2)}, u32[]{:S(2)}) async-start(f32[4,80,512]{2,1,0:T(8,128)} %get-tuple-element.10), calls=%async_computation.2 | async-start | bytes 1310720 | tf_op jit(solution)/shard_map/all_to_all | solution.py:347
  61.3 0.6 reduce.1
  61.9 9.3 %all-to-all-done.2.received_ref = f32[4,80,512]{2,1,0:T(8,128)S(1)} async-done(((f32[4,80,512]{2,1,0:T(8,128)}), f32[4,80,512]{2,1,0:T(8,128)S(1)}, u32[]{:S(2)}, u32[]{:S(2)}) %all-to-all-start.2) | async-done | bytes 655392 | tf_op jit(solution)/shard_map/all_to_all | solution.py:347
  71.2 0.0 copy-done.1
  71.2 1.0 %divide.1 = f32[288,128]{1,0:T(8,128)} custom-call(s32[1]{0:T(128)} %bitcast.share_ref, f32[4,80,512]{2,1,0:T(8,128)S(1)} %all-to-all-done.2.received_ref, f32[64,2048]{1,0:T(8,128)S(1)} %copy-done.1), custom_call_target="tpu_custom_call" | custom-call | tf_op jit(solution)/shard_map/divide/pallas_call | solution.py:329
  (4 shorter events, 0.1 us)
Async XLA Ops:
  2.7 1.0 %copy-start = (f32[64,2048]{1,0:T(8,128)S(1)}, f32[64,2048]{1,0:T(8,128)}, u32[]{:S(2)}) copy-start(f32[64,2048]{1,0:T(8,128)} %noise_ref.3) | copy-start | bytes 1572868
  3.8 1.0 %copy-start.2 = (bf16[36,2,2048]{2,1,0:T(2,128)(2,1)S(1)}, bf16[36,2,2048]{2,1,0:T(2,128)(2,1)}, u32[]{:S(2)}) copy-start(bf16[36,2,2048]{2,1,0:T(2,128)(2,1)} %param.9) | copy-start | bytes 884740
  4.8 0.8 %copy-start.3 = (f32[8,2048]{1,0:T(8,128)S(1)}, f32[8,2048]{1,0:T(8,128)}, u32[]{:S(2)}) copy-start(f32[8,2048]{1,0:T(8,128)} %constant.10.clone.phase_ref) | copy-start | bytes 196612
  5.6 0.7 copy-start.5
  6.3 48.1 %copy-start.4 = (f32[8,2048]{1,0:T(8,128)S(1)}, f32[8,2048]{1,0:T(8,128)}, u32[]{:S(2)}) copy-start(f32[8,2048]{1,0:T(8,128)} %constant.10.clone.phase_ref) | copy-start | bytes 196612
  16.3 54.9 %copy-start.1 = (f32[64,2048]{1,0:T(8,128)S(1)}, f32[64,2048]{1,0:T(8,128)}, u32[]{:S(2)}) copy-start(f32[64,2048]{1,0:T(8,128)} %noise_ref.3) | copy-start | bytes 1572868
  57.1 14.1 %all-to-all-start.2 = ((f32[4,80,512]{2,1,0:T(8,128)}), f32[4,80,512]{2,1,0:T(8,128)S(1)}, u32[]{:S(2)}, u32[]{:S(2)}) async-start(f32[4,80,512]{2,1,0:T(8,128)} %get-tuple-element.10), calls=%async_computation.2 | async-start | bytes 1310720 | tf_op jit(solution)/shard_map/all_to_all | solution.py:347

commit v3 on v2

--- a/solution.py
+++ b/solution.py
@@ -15,7 +15,8 @@
 PAIRS = (5, 6, 7, 8)
 LOWEST = -1.0e30
 HIGHEST = lax.Precision.HIGHEST
-VMEM_BYTES = 50 * 1024 * 1024
+SCORE_VMEM = 36 * 1024 * 1024
+OTHER_VMEM = 24 * 1024 * 1024
 
 
 def phase_tables(coeffs):
@@ -48,6 +49,17 @@
 
 
 def score_kernel(
+    images_hbm,
+    refs_hbm,
+    noise_hbm,
+    prior_hbm,
+    groups_hbm,
+    prior_index_hbm,
+    class_hbm,
+    phase_hbm,
+    scores_ref,
+    weighted_ref,
+    partial_ref,
     images_ref,
     refs_ref,
     noise_ref,
@@ -56,47 +68,65 @@
     prior_index_ref,
     class_ref,
     phase_ref,
-    scores_ref,
-    weighted_ref,
-    partial_ref,
-    images_vmem,
     image_wide,
     ref_wide,
     shifted,
     weights,
     power,
-    image_sem,
+    sems,
 ):
-    particles = groups_ref.shape[1]
+    particles = groups_ref.shape[0]
     coeffs = noise_ref.shape[1]
     ngroups = noise_ref.shape[0]
     blocks = coeffs // LANES
     orients = class_ref.shape[0]
     padded = (orients + 7) // 8 * 8
-    stride = 2 * blocks
-    fetch = pltpu.make_async_copy(images_ref, images_vmem, image_sem)
-    fetch.start()
-
-    ref_wide[0 : orients * stride, :] = refs_ref[...].astype(jnp.float32)
-    ref_wide[orients * stride :, :] = jnp.zeros(
-        ((padded - orients) * stride, LANES), jnp.float32
-    )
-    group_hot = hot_columns(ngroups, groups_ref[...])
-    group_bf16 = group_hot.astype(jnp.float32).astype(jnp.bfloat16)
-    noise_parts = jnp.concatenate(split_bf16(noise_ref[...]), axis=0)
-    weights[...] = lax.dot_general(
-        jnp.concatenate([group_bf16] * 3, axis=0),
-        noise_parts,
-        (((0,), (0,)), ((), ())),
-        preferred_element_type=jnp.float32,
-    )
-
+    rows = 2 * blocks
+    pitch = rows + 1
+    pairs = (
+        (refs_hbm, refs_ref),
+        (phase_hbm, phase_ref),
+        (groups_hbm, groups_ref),
+        (noise_hbm, noise_ref),
+        (prior_index_hbm, prior_index_ref),
+        (class_hbm, class_ref),
+        (prior_hbm, prior_ref),
+        (images_hbm, images_ref),
+    )
+    fetches = [pltpu.make_async_copy(*pair, sems.at[i]) for i, pair in enumerate(pairs)]
+    for fetch in fetches:
+        fetch.start()
+    for fetch in fetches[:3]:
+        fetch.wait()
+    tables = 9 * padded + 8 + ngroups
+    for b in range(blocks):
+        scores_ref[tables + 8 * b : tables + 8 * b + 8, 0:LANES] = phase_ref[
+            :, b * LANES : (b + 1) * LANES
+        ]
+
+    def spread(source, target, first, count):
+        for k in range(count):
+            wide = source[pl.ds((first + k) * rows, rows), :].astype(jnp.float32)
+            for step in range(0, rows, 8):
+                target[pl.ds(pl.multiple_of(first * pitch, 8) + k * pitch + step, 8), :] = wide[
+                    step : step + 8
+                ]
+
+    for first in range(0, orients, 8):
+        spread(refs_ref, ref_wide, first, min(8, orients - first))
+    ref_wide[orients * pitch :, :] = jnp.zeros(
+        (ref_wide.shape[0] - orients * pitch, LANES), jnp.float32
+    )
+    group_hot = hot_columns(ngroups, groups_ref[...].reshape(1, particles))
+    group_hot = group_hot.astype(jnp.float32)
+    scores_ref[9 * padded + 8 : tables] = group_hot
+    group_hot = group_hot.astype(jnp.bfloat16)
     @pl.loop(0, blocks)
     def _(b):
         here = pl.ds(pl.multiple_of(b * LANES, LANES), LANES)
-        real = ref_wide[pl.ds(2 * b, padded, stride=stride), :]
-        imag = ref_wide[pl.ds(2 * b + 1, padded, stride=stride), :]
-        power[:, here] = real * real + imag * imag
+        real = ref_wide[pl.ds(2 * b, padded, stride=pitch), :]
+        imag = ref_wide[pl.ds(2 * b + 1, padded, stride=pitch), :]
+        power[:, here] = jnp.concatenate(split_bf16(real * real + imag * imag), axis=0)
         reals = [real, jnp.zeros((8, LANES), jnp.float32)]
         imags = [imag, jnp.zeros((8, LANES), jnp.float32)]
         for k in range(4):
@@ -112,46 +142,51 @@
             jnp.bfloat16
         )
 
-    quadratic = lax.dot_general(
-        power[...],
-        noise_ref[...],
-        (((1,), (1,)), ((), ())),
+    fetches[3].wait()
+    noise_parts = jnp.concatenate(split_bf16(noise_ref[...]), axis=0)
+    weights[...] = lax.dot_general(
+        jnp.concatenate([group_hot] * 3, axis=0),
+        noise_parts,
+        (((0,), (0,)), ((), ())),
+        preferred_element_type=jnp.float32,
+    )
+    products = lax.dot_general(
+        power[...], noise_parts, (((1,), (1,)), ((), ())), preferred_element_type=jnp.float32
+    )
+    products = products[0:padded] + products[padded : 2 * padded] + products[2 * padded :]
+    quadratic = (
+        products[:, 0:ngroups]
+        + products[:, ngroups : 2 * ngroups]
+        + products[:, 2 * ngroups : 3 * ngroups]
+    )
+    for fetch in fetches[4:7]:
+        fetch.wait()
+    class_hot = hot_columns(prior_ref.shape[1], class_ref[...].reshape(1, orients))
+    class_prior = lax.dot_general(
+        class_hot.astype(jnp.float32),
+        prior_ref[...],
+        (((0,), (1,)), ((), ())),
         precision=HIGHEST,
         preferred_element_type=jnp.float32,
     )
-    classes = prior_ref.shape[1]
-    class_hot = (
-        lax.broadcasted_iota(jnp.int32, (orients, classes), 1) == class_ref[...]
-    ).astype(jnp.float32)
-    class_hot = jnp.concatenate(
-        [class_hot, jnp.zeros((padded - orients, classes), jnp.float32)], axis=0
-    )
-    class_prior = lax.dot_general(
-        class_hot,
-        prior_ref[...],
-        (((1,), (1,)), ((), ())),
-        precision=HIGHEST,
+    class_prior = jnp.concatenate(
+        [class_prior, jnp.zeros((padded - orients, prior_ref.shape[0]), jnp.float32)], axis=0
+    )
+    prior_hot = hot_columns(prior_ref.shape[0], prior_index_ref[...].reshape(1, particles))
+    prior_hot = prior_hot.astype(jnp.float32)
+    offsets = jnp.dot(
+        jnp.concatenate(split_bf16(-0.5 * quadratic), axis=1),
+        jnp.concatenate([group_hot] * 3, axis=0),
         preferred_element_type=jnp.float32,
-    )
-    prior_hot = hot_columns(prior_ref.shape[0], prior_index_ref[...]).astype(jnp.float32)
-    offsets = jnp.dot(
-        class_prior, prior_hot, precision=HIGHEST, preferred_element_type=jnp.float32
-    ) - 0.5 * jnp.dot(
-        quadratic,
-        group_hot.astype(jnp.float32),
-        precision=HIGHEST,
-        preferred_element_type=jnp.float32,
-    )
+    ) + jnp.dot(class_prior, prior_hot, precision=HIGHEST, preferred_element_type=jnp.float32)
     real_row = lax.broadcasted_iota(jnp.int32, (padded, particles), 0) < orients
     offsets = jnp.where(real_row, offsets, LOWEST)
 
-    fetch.wait()
-
-    @pl.loop(0, blocks)
-    def _(b):
-        part = particles // blocks * stride
-        rows = pl.ds(pl.multiple_of(b * part, part), part)
-        image_wide[rows, :] = images_vmem[rows, :].astype(jnp.float32)
+    fetches[7].wait()
+
+    @pl.loop(0, particles // 8)
+    def _(g):
+        spread(images_ref, image_wide, g * 8, 8)
 
     @pl.loop(0, blocks)
     def _(b):
@@ -159,7 +194,7 @@
         weight = weights[:, here]
         wide = pl.multiple_of(b * 2 * LANES, 2 * LANES)
         for part in range(2):
-            picked = image_wide[pl.ds(2 * b + part, particles, stride=stride), :]
+            picked = image_wide[pl.ds(2 * b + part, particles, stride=pitch), :]
             weighted_ref[:, pl.ds(wide + part * LANES, LANES)] = (picked * weight).astype(
                 jnp.bfloat16
             )
@@ -173,20 +208,25 @@
     scores = correlation + jnp.concatenate(
         [offsets, jnp.full((8, particles), LOWEST, jnp.float32)] + [offsets] * 8, axis=0
     )
-    scores_ref[...] = scores
+    scores_ref[0 : 9 * padded + 8] = scores
     partial_ref[...] = jnp.broadcast_to(log_sum(scores)[None], partial_ref.shape)
 
 
 def update_kernel(
-    partial_ref, scores_ref, weighted_ref, groups_ref, phase_ref, ngroups, likelihood_ref, out_ref
+    ngroups, partial_ref, scores_ref, weighted_ref, likelihood_ref, out_hbm, out_ref, sems
 ):
     orients = (out_ref.shape[1] - 8) // 2
     padded = (orients + 7) // 8 * 8
     width = out_ref.shape[2]
+    stores = [
+        pltpu.make_async_copy(out_ref.at[share], out_hbm.at[share], sems.at[share])
+        for share in range(out_ref.shape[0])
+    ]
     likelihood = log_sum(partial_ref[:, 0, :])
     likelihood_ref[...] = likelihood
-    posterior = jnp.exp(scores_ref[...] - likelihood).astype(jnp.bfloat16)
-    group_hot = hot_columns(ngroups, groups_ref[...]).astype(jnp.float32).astype(jnp.bfloat16)
+    rows = 9 * padded + 8
+    posterior = jnp.exp(scores_ref[0:rows] - likelihood).astype(jnp.bfloat16)
+    group_hot = scores_ref[rows : rows + ngroups].astype(jnp.bfloat16)
     mass = lax.dot_general(
         posterior, group_hot, (((1,), (1,)), ((), ())), preferred_element_type=jnp.float32
     )
@@ -200,7 +240,7 @@
         out_ref[share, 2 * orients :, :] = mass_rows
         for step in range(width // LANES):
             b = share * (width // LANES) + step
-            here = slice(b * LANES, (b + 1) * LANES)
+            table = rows + ngroups + 8 * b
             product = jnp.dot(
                 posterior,
                 weighted_ref[:, 2 * b * LANES : 2 * (b + 1) * LANES],
@@ -209,8 +249,8 @@
             real = product[0:padded, 0:LANES]
             imag = product[0:padded, LANES:]
             for k in range(4):
-                cosine = phase_ref[k : k + 1, here]
-                sine = phase_ref[k + 4 : k + 5, here]
+                cosine = scores_ref[table + k : table + k + 1, 0:LANES]
+                sine = scores_ref[table + k + 4 : table + k + 5, 0:LANES]
                 low = 48 + 2 * padded * k
                 ahead = product[low : low + padded]
                 behind = product[low + padded : low + 2 * padded]
@@ -220,6 +260,9 @@
             there = slice(step * LANES, (step + 1) * LANES)
             out_ref[share, 0:orients, there] = real[0:orients]
             out_ref[share, orients : 2 * orients, there] = imag[0:orients]
+        stores[share].start()
+    for store in stores:
+        store.wait()
 
 
 def divide_kernel(share_ref, received_ref, noise_ref, out_ref):
@@ -258,8 +301,8 @@
     )
 
 
-def kernel_params():
-    return pltpu.CompilerParams(vmem_limit_bytes=VMEM_BYTES)
+def kernel_params(limit):
+    return pltpu.CompilerParams(vmem_limit_bytes=limit)
 
 
 def score_call(images, references, noise_weights, log_prior, groups, prior_index, class_map, phase, spread):
@@ -267,59 +310,61 @@
     orients = references.shape[0]
     padded = (orients + 7) // 8 * 8
     rows = 9 * padded + 8
-    whole = pl.BlockSpec(memory_space=pltpu.VMEM)
-    return pl.pallas_call(
-        score_kernel,
-        in_specs=[pl.BlockSpec(memory_space=pl.ANY)] + [whole] * 7,
-        out_specs=[whole] * 3,
-        out_shape=[
-            jax.ShapeDtypeStruct((rows, particles), jnp.float32),
-            jax.ShapeDtypeStruct((particles, 2 * coeffs), jnp.bfloat16),
-            jax.ShapeDtypeStruct((spread, 1, particles), jnp.float32),
-        ],
-        scratch_shapes=[
-            pltpu.VMEM((particles * 2 * coeffs // LANES, LANES), jnp.bfloat16),
-            pltpu.VMEM((particles * 2 * coeffs // LANES, LANES), jnp.float32),
-            pltpu.VMEM((padded * 2 * coeffs // LANES, LANES), jnp.float32),
-            pltpu.VMEM((rows, 2 * coeffs), jnp.bfloat16),
-            pltpu.VMEM((particles, coeffs), jnp.float32),
-            pltpu.VMEM((padded, coeffs), jnp.float32),
-            pltpu.SemaphoreType.DMA,
-        ],
-        compiler_params=kernel_params(),
-        name="score",
-    )(
+    ngroups = noise_weights.shape[0]
+    operands = [
         rows_of(images),
         rows_of(references),
         noise_weights,
         log_prior,
-        groups[None, :],
-        prior_index[None, :],
-        class_map[:, None],
+        groups,
+        prior_index,
+        class_map,
         phase,
-    )
-
-
-def update_call(partials, scores, weighted, groups, phase, ngroups, orients, shares):
+    ]
+    return pl.pallas_call(
+        score_kernel,
+        in_specs=[pl.BlockSpec(memory_space=pltpu.HBM)] * 8,
+        out_specs=[pl.BlockSpec(memory_space=pltpu.VMEM)] * 3,
+        out_shape=[
+            pltpu.VMEM((rows + ngroups + 8 * coeffs // LANES, particles), jnp.float32),
+            pltpu.VMEM((particles, 2 * coeffs), jnp.bfloat16),
+            jax.ShapeDtypeStruct((spread, 1, particles), jnp.float32),
+        ],
+        scratch_shapes=[pltpu.VMEM(array.shape, array.dtype) for array in operands]
+        + [
+            pltpu.VMEM((particles * (2 * coeffs // LANES + 1), LANES), jnp.float32),
+            pltpu.VMEM((padded * (2 * coeffs // LANES + 1), LANES), jnp.float32),
+            pltpu.VMEM((rows, 2 * coeffs), jnp.bfloat16),
+            pltpu.VMEM((particles, coeffs), jnp.float32),
+            pltpu.VMEM((3 * padded, coeffs), jnp.bfloat16),
+            pltpu.SemaphoreType.DMA((8,)),
+        ],
+        compiler_params=kernel_params(SCORE_VMEM),
+        name="score",
+    )(*[pltpu.with_memory_space_constraint(array, pltpu.HBM) for array in operands])
+
+
+def update_call(partials, scores, weighted, ngroups, orients, shares):
     particles, wide = weighted.shape
+    block = (shares, 2 * orients + 8, wide // 2 // shares)
+    kept = [
+        pltpu.with_memory_space_constraint(array, pltpu.VMEM)
+        for array in (scores, weighted)
+    ]
     whole = pl.BlockSpec(memory_space=pltpu.VMEM)
 
-    def body(partial_ref, scores_ref, weighted_ref, groups_ref, phase_ref, likelihood_ref, out_ref):
-        update_kernel(
-            partial_ref, scores_ref, weighted_ref, groups_ref, phase_ref, ngroups, likelihood_ref, out_ref
-        )
-
     return pl.pallas_call(
-        body,
-        in_specs=[whole] * 5,
-        out_specs=[whole] * 2,
+        functools.partial(update_kernel, ngroups),
+        in_specs=[whole] * 3,
+        out_specs=[whole, pl.BlockSpec(memory_space=pltpu.HBM)],
         out_shape=[
             jax.ShapeDtypeStruct((1, particles), jnp.float32),
-            jax.ShapeDtypeStruct((shares, 2 * orients + 8, wide // 2 // shares), jnp.float32),
+            pltpu.HBM(block, jnp.float32),
         ],
-        compiler_params=kernel_params(),
+        scratch_shapes=[pltpu.VMEM(block, jnp.float32), pltpu.SemaphoreType.DMA((shares,))],
+        compiler_params=kernel_params(OTHER_VMEM),
         name="update",
-    )(partials, scores, weighted, groups[None, :], phase)
+    )(partials, *kept)
 
 
 def divide_call(share, received, noise_weights):
@@ -338,9 +383,13 @@
             out_specs=pl.BlockSpec((orients * 2 * width // LANES, LANES), lambda i, s: (0, 0)),
         ),
         out_shape=jax.ShapeDtypeStruct((orients * 2 * width // LANES, LANES), jnp.float32),
-        compiler_params=kernel_params(),
+        compiler_params=kernel_params(OTHER_VMEM),
         name="divide",
-    )(share, received, noise_weights)
+    )(
+        share,
+        pltpu.with_memory_space_constraint(received, pltpu.VMEM),
+        pltpu.with_memory_space_constraint(noise_weights, pltpu.HBM),
+    )
 
 
 def exchange(spread, axes):
@@ -361,7 +410,7 @@
     partial = jnp.broadcast_to(partial[None], (plane, 1, partial.shape[1]))
     partials = exchange(partial, ("x", "core"))
     likelihood, blocks = update_call(
-        partials, scores, weighted, groups, phase, noise_weights.shape[0], orients, shares
+        partials, scores, weighted, noise_weights.shape[0], orients, shares
     )
     received = exchange(blocks, "dom")
     share = lax.axis_index("dom").astype(jnp.int32)[None]

time: 72.6 us -> 64.2 us (0.88)
  local copies, waits for them, and re-layouts: 5.66 us -> 0.01 us
  Pallas kernels: 13.7 us -> 11.3 us
    unnamed x12 -> x0, local copies, waits for them, and re-layouts: 3.54 us -> none
    pallas_call x2, Pallas kernels: 12.8 us -> 9.45 us  [the longest x1 6.86 us: score_call(): pl.pallas_call(score_kernel, in_specs=[pl.BlockSpec(memory_space=pltpu.HB...]
    broadcast_in_dim x3 -> x0, local copies, waits for them, and re-layouts: 2.12 us -> none  [the longest x1 0.75 us: score_call(): class_map[:, None]]
    pallas_call x1, Pallas kernels: 0.97 us -> 1.87 us  [divide_call(): pl.pallas_call(divide_kernel, grid_spec=pltpu.PrefetchScalarGridSpec(num_...]
where the time goes in v3:
time: 64.2 us; the launch traced here: 64 us
  blocking collectives  37.8 us (59%)
  Pallas kernels  11.3 us (18%)
  waiting for transfers between devices  9.34 us (15%)
  starting transfers between devices  4.2 us (7%)
  other arithmetic  0.67 us (1%)
  between operations  0.66 us (1%)
    all_to_all x2, blocking collectives, exchange(): return lax.all_to_all(spread, axes, 0, 0, tiled=True)  37.8 us
    all_to_all x1, waiting for transfers between devices, exchange(): return lax.all_to_all(spread, axes, 0, 0, tiled=True)  9.34 us
    pallas_call x1, Pallas kernels, score_call(): pl.pallas_call(score_kernel, in_specs=[pl.BlockSpec(memory_space=pltpu.HB...  6.86 us
    all_to_all x1, starting transfers between devices, exchange(): return lax.all_to_all(spread, axes, 0, 0, tiled=True)  4.2 us
    pallas_call x1, Pallas kernels, update_call(): pl.pallas_call(functools.partial(update_kernel, ngroups), in_specs=[whole...  2.59 us
    pallas_call x1, Pallas kernels, divide_call(): pl.pallas_call(divide_kernel, grid_spec=pltpu.PrefetchScalarGridSpec(num_...  1.87 us
  transfers between devices with their start and end apart: 1, of which 1 were waited for; matrix products, arithmetic and copies ran while one was open for 1% of the time, Pallas kernels for 0%

profile of v3, /device:TPU:1, one launch (start us, length us, event | category | flops | bytes accessed | tf_op | source)
XLA Modules:
  0.0 64.0 jit_solution(14211121396007956674)
XLA Ops:
  0.6 6.9 %score.1 = (f32[560,288]{1,0:T(8,128)S(1)}, bf16[288,4096]{1,0:T(8,128)(2,1)S(1)}, f32[16,1,288]{2,1,0:T(1,128)S(1)}) custom-call(bf16[9216,128]{1,0:T(8,128)(2,1)} %bitcast.22, bf16[1152,128]{1,0:T(8,128)(2,1)} %bitcast.23, f32[64,2048]{1,0:T(8,128)} %noise_ref.1, f32[8,16]{1,0:T(8,128)} %prior_hbm.1, s32[288]{0:T(512)} %groups_hbm.1, s32[288]{0:T(512)} %prior_index_hbm.1, ...), custom_call_target="tpu_custom_call" | custom-call | tf_op jit(solution)/shard_map/score/pallas_call | solution.py:324
  7.5 27.0 %all_to_all.15 = f32[16,1,288]{2,1,0:T(1,128)S(1)} all-to-all(f32[16,1,288]{2,1,0:T(1,128)S(1)} %get-tuple-element.7), channel_id=1, replica_groups=mesh['z'=16,'x'=4,'core'=2,'dom'=4] {'z'}, dimensions={0} | all-to-all | bytes 36864 | tf_op jit(solution)/shard_map/all_to_all | solution.py:396
  34.6 10.8 %all_to_all.16.partial_ref = f32[8,1,288]{2,1,0:T(1,128)S(1)} all-to-all(f32[8,1,288]{2,1,0:T(1,128)S(1)} %broadcast_in_dim.5), channel_id=1, replica_groups=mesh['z'=16,'x'=4,'core'=2,'dom'=4] {'x','core'}, dimensions={0} | all-to-all | bytes 18432 | tf_op jit(solution)/shard_map/all_to_all | solution.py:396
  45.4 2.6 %update.1 = (f32[1,288]{1,0:T(1,128)S(1)}, f32[4,80,512]{2,1,0:T(8,128)}) custom-call(f32[8,1,288]{2,1,0:T(1,128)S(1)} %all_to_all.16.partial_ref, f32[560,288]{1,0:T(8,128)S(1)} %get-tuple-element.8.scores_ref, bf16[288,4096]{1,0:T(8,128)(2,1)S(1)} %get-tuple-element.9.weighted_ref), custom_call_target="tpu_custom_call" | custom-call | tf_op jit(solution)/shard_map/update/pallas_call | solution.py:356
  48.0 4.2 %all-to-all-start.2 = ((f32[4,80,512]{2,1,0:T(8,128)}), f32[4,80,512]{2,1,0:T(8,128)S(1)}, u32[]{:S(2)}, u32[]{:S(2)}) async-start(f32[4,80,512]{2,1,0:T(8,128)} %get-tuple-element.10), calls=%async_computation.2 | async-start | bytes 1310720 | tf_op jit(solution)/shard_map/all_to_all | solution.py:396
  52.2 0.6 reduce.1
  52.8 9.3 %all-to-all-done.2.received_ref = f32[4,80,512]{2,1,0:T(8,128)S(1)} async-done(((f32[4,80,512]{2,1,0:T(8,128)}), f32[4,80,512]{2,1,0:T(8,128)S(1)}, u32[]{:S(2)}, u32[]{:S(2)}) %all-to-all-start.2) | async-done | bytes 655392 | tf_op jit(solution)/shard_map/all_to_all | solution.py:396
  62.1 1.9 %divide.1 = f32[288,128]{1,0:T(8,128)} custom-call(s32[1]{0:T(128)} %bitcast.share_ref, f32[4,80,512]{2,1,0:T(8,128)S(1)} %all-to-all-done.2.received_ref, f32[64,2048]{1,0:T(8,128)} %noise_ref.1), custom_call_target="tpu_custom_call" | custom-call | tf_op jit(solution)/shard_map/divide/pallas_call | solution.py:374
  (4 shorter events, 0.1 us)
Async XLA Ops:
  48.0 14.1 %all-to-all-start.2 = ((f32[4,80,512]{2,1,0:T(8,128)}), f32[4,80,512]{2,1,0:T(8,128)S(1)}, u32[]{:S(2)}, u32[]{:S(2)}) async-start(f32[4,80,512]{2,1,0:T(8,128)} %get-tuple-element.10), calls=%async_computation.2 | async-start | bytes 1310720 | tf_op jit(solution)/shard_map/all_to_all | solution.py:396

commit v4 on v3

--- a/solution.py
+++ b/solution.py
@@ -121,9 +121,16 @@
     group_hot = group_hot.astype(jnp.float32)
     scores_ref[9 * padded + 8 : tables] = group_hot
     group_hot = group_hot.astype(jnp.bfloat16)
-    @pl.loop(0, blocks)
-    def _(b):
-        here = pl.ds(pl.multiple_of(b * LANES, LANES), LANES)
+    fetches[3].wait()
+    noise_parts = jnp.concatenate(split_bf16(noise_ref[...]), axis=0)
+    weights[...] = lax.dot_general(
+        jnp.concatenate([group_hot] * 3, axis=0),
+        noise_parts,
+        (((0,), (0,)), ((), ())),
+        preferred_element_type=jnp.float32,
+    )
+    for b in range(blocks):
+        here = pl.ds(b * LANES, LANES)
         real = ref_wide[pl.ds(2 * b, padded, stride=pitch), :]
         imag = ref_wide[pl.ds(2 * b + 1, padded, stride=pitch), :]
         power[:, here] = jnp.concatenate(split_bf16(real * real + imag * imag), axis=0)
@@ -136,20 +143,12 @@
             imag_cos, imag_sin = imag * cosine, imag * sine
             reals += [real_cos + imag_sin, real_cos - imag_sin]
             imags += [imag_cos - real_sin, imag_cos + real_sin]
-        wide = pl.multiple_of(b * 2 * LANES, 2 * LANES)
+        wide = b * 2 * LANES
         shifted[:, pl.ds(wide, LANES)] = jnp.concatenate(reals, axis=0).astype(jnp.bfloat16)
         shifted[:, pl.ds(wide + LANES, LANES)] = jnp.concatenate(imags, axis=0).astype(
             jnp.bfloat16
         )
 
-    fetches[3].wait()
-    noise_parts = jnp.concatenate(split_bf16(noise_ref[...]), axis=0)
-    weights[...] = lax.dot_general(
-        jnp.concatenate([group_hot] * 3, axis=0),
-        noise_parts,
-        (((0,), (0,)), ((), ())),
-        preferred_element_type=jnp.float32,
-    )
     products = lax.dot_general(
         power[...], noise_parts, (((1,), (1,)), ((), ())), preferred_element_type=jnp.float32
     )
@@ -182,32 +181,34 @@
     real_row = lax.broadcasted_iota(jnp.int32, (padded, particles), 0) < orients
     offsets = jnp.where(real_row, offsets, LOWEST)
 
+    scores_ref[0 : 9 * padded + 8] = jnp.concatenate(
+        [offsets, jnp.full((8, particles), LOWEST, jnp.float32)] + [offsets] * 8, axis=0
+    )
     fetches[7].wait()
 
-    @pl.loop(0, particles // 8)
+    @pl.loop(0, particles // 32)
     def _(g):
-        spread(images_ref, image_wide, g * 8, 8)
-
-    @pl.loop(0, blocks)
-    def _(b):
-        here = pl.ds(pl.multiple_of(b * LANES, LANES), LANES)
-        weight = weights[:, here]
-        wide = pl.multiple_of(b * 2 * LANES, 2 * LANES)
-        for part in range(2):
-            picked = image_wide[pl.ds(2 * b + part, particles, stride=pitch), :]
-            weighted_ref[:, pl.ds(wide + part * LANES, LANES)] = (picked * weight).astype(
-                jnp.bfloat16
-            )
-
-    correlation = lax.dot_general(
-        shifted[...],
-        weighted_ref[...],
-        (((1,), (1,)), ((), ())),
-        preferred_element_type=jnp.float32,
-    )
-    scores = correlation + jnp.concatenate(
-        [offsets, jnp.full((8, particles), LOWEST, jnp.float32)] + [offsets] * 8, axis=0
-    )
+        for h in range(4):
+            spread(images_ref, image_wide, g * 32 + h * 8, 8)
+
+    total = None
+    for b in range(blocks):
+        weight = weights[:, pl.ds(b * LANES, LANES)]
+        wide = pl.ds(b * 2 * LANES, 2 * LANES)
+        both = [
+            image_wide[pl.ds(2 * b + part, particles, stride=pitch), :] * weight
+            for part in range(2)
+        ]
+        both = jnp.concatenate(both, axis=1).astype(jnp.bfloat16)
+        weighted_ref[:, wide] = both
+        product = lax.dot_general(
+            shifted[:, wide],
+            both,
+            (((1,), (1,)), ((), ())),
+            preferred_element_type=jnp.float32,
+        )
+        total = product if total is None else total + product
+    scores = scores_ref[0 : 9 * padded + 8] + total
     scores_ref[0 : 9 * padded + 8] = scores
     partial_ref[...] = jnp.broadcast_to(log_sum(scores)[None], partial_ref.shape)
 
@@ -404,11 +405,11 @@
     plane = lax.axis_size("x") * lax.axis_size("core")
     shares = lax.axis_size("dom")
     scores, weighted, partial = score_call(
-        images, references, noise_weights, log_prior, groups, prior_index, class_map, phase, depth
-    )
-    partial = log_sum(exchange(partial, "z")[:, 0, :])
-    partial = jnp.broadcast_to(partial[None], (plane, 1, partial.shape[1]))
-    partials = exchange(partial, ("x", "core"))
+        images, references, noise_weights, log_prior, groups, prior_index, class_map, phase, plane
+    )
+    partial = log_sum(exchange(partial, ("x", "core"))[:, 0, :])
+    partial = jnp.broadcast_to(partial[None], (depth, 1, partial.shape[1]))
+    partials = exchange(partial, "z")
     likelihood, blocks = update_call(
         partials, scores, weighted, noise_weights.shape[0], orients, shares
     )

time: 64.2 us -> 61.1 us (0.952)
  the two profiles are of different devices: /device:TPU:1 before, /device:TPU:2 now
where the time goes in v4:
time: 61.1 us; the launch traced here: 60.8 us
  blocking collectives  36.1 us (59%)
  Pallas kernels  10.1 us (17%)
  waiting for transfers between devices  8.83 us (14%)
  starting transfers between devices  4.47 us (7%)
  between operations  0.67 us (1%)
  other arithmetic  0.65 us (1%)
    all_to_all x2, blocking collectives, exchange(): return lax.all_to_all(spread, axes, 0, 0, tiled=True)  36.1 us
    all_to_all x1, waiting for transfers between devices, exchange(): return lax.all_to_all(spread, axes, 0, 0, tiled=True)  8.83 us
    pallas_call x1, Pallas kernels, score_call(): pl.pallas_call(score_kernel, in_specs=[pl.BlockSpec(memory_space=pltpu.HB...  5.62 us
    all_to_all x1, starting transfers between devices, exchange(): return lax.all_to_all(spread, axes, 0, 0, tiled=True)  4.47 us
    pallas_call x1, Pallas kernels, update_call(): pl.pallas_call(functools.partial(update_kernel, ngroups), in_specs=[whole...  2.6 us
    pallas_call x1, Pallas kernels, divide_call(): pl.pallas_call(divide_kernel, grid_spec=pltpu.PrefetchScalarGridSpec(num_...  1.87 us
  transfers between devices with their start and end apart: 1, of which 1 were waited for; matrix products, arithmetic and copies ran while one was open for 1% of the time, Pallas kernels for 0%

profile of v4, /device:TPU:2, one launch (start us, length us, event | category | flops | bytes accessed | tf_op | source)
XLA Modules:
  0.0 60.8 jit_solution(2197741068494197779)
XLA Ops:
  0.6 5.6 %score.1 = (f32[560,288]{1,0:T(8,128)S(1)}, bf16[288,4096]{1,0:T(8,128)(2,1)S(1)}, f32[8,1,288]{2,1,0:T(1,128)S(1)}) custom-call(bf16[9216,128]{1,0:T(8,128)(2,1)} %bitcast.22, bf16[1152,128]{1,0:T(8,128)(2,1)} %bitcast.23, f32[64,2048]{1,0:T(8,128)} %noise_ref.1, f32[8,16]{1,0:T(8,128)} %prior_hbm.1, s32[288]{0:T(512)} %groups_hbm.1, s32[288]{0:T(512)} %prior_index_hbm.1, ...), custom_call_target="tpu_custom_call" | custom-call | tf_op jit(solution)/shard_map/score/pallas_call | solution.py:325
  6.3 12.1 %all_to_all.15 = f32[8,1,288]{2,1,0:T(1,128)S(1)} all-to-all(f32[8,1,288]{2,1,0:T(1,128)S(1)} %get-tuple-element.7), channel_id=1, replica_groups=mesh['z'=16,'x'=4,'core'=2,'dom'=4] {'x','core'}, dimensions={0} | all-to-all | bytes 18432 | tf_op jit(solution)/shard_map/all_to_all | solution.py:397
  18.5 23.9 %all_to_all.16.partial_ref = f32[16,1,288]{2,1,0:T(1,128)S(1)} all-to-all(f32[16,1,288]{2,1,0:T(1,128)S(1)} %broadcast_in_dim.5), channel_id=1, replica_groups=mesh['z'=16,'x'=4,'core'=2,'dom'=4] {'z'}, dimensions={0} | all-to-all | bytes 36864 | tf_op jit(solution)/shard_map/all_to_all | solution.py:397
  42.4 2.6 %update.1 = (f32[1,288]{1,0:T(1,128)S(1)}, f32[4,80,512]{2,1,0:T(8,128)}) custom-call(f32[16,1,288]{2,1,0:T(1,128)S(1)} %all_to_all.16.partial_ref, f32[560,288]{1,0:T(8,128)S(1)} %get-tuple-element.8.scores_ref, bf16[288,4096]{1,0:T(8,128)(2,1)S(1)} %get-tuple-element.9.weighted_ref), custom_call_target="tpu_custom_call" | custom-call | tf_op jit(solution)/shard_map/update/pallas_call | solution.py:357
  45.0 4.5 %all-to-all-start.2 = ((f32[4,80,512]{2,1,0:T(8,128)}), f32[4,80,512]{2,1,0:T(8,128)S(1)}, u32[]{:S(2)}, u32[]{:S(2)}) async-start(f32[4,80,512]{2,1,0:T(8,128)} %get-tuple-element.10), calls=%async_computation.2 | async-start | bytes 1310720 | tf_op jit(solution)/shard_map/all_to_all | solution.py:397
  49.5 0.6 reduce.1
  50.1 8.8 %all-to-all-done.2.received_ref = f32[4,80,512]{2,1,0:T(8,128)S(1)} async-done(((f32[4,80,512]{2,1,0:T(8,128)}), f32[4,80,512]{2,1,0:T(8,128)S(1)}, u32[]{:S(2)}, u32[]{:S(2)}) %all-to-all-start.2) | async-done | bytes 655392 | tf_op jit(solution)/shard_map/all_to_all | solution.py:397
  58.9 1.9 %divide.1 = f32[288,128]{1,0:T(8,128)} custom-call(s32[1]{0:T(128)} %bitcast.share_ref, f32[4,80,512]{2,1,0:T(8,128)S(1)} %all-to-all-done.2.received_ref, f32[64,2048]{1,0:T(8,128)} %noise_ref.1), custom_call_target="tpu_custom_call" | custom-call | tf_op jit(solution)/shard_map/divide/pallas_call | solution.py:375
  (4 shorter events, 0.1 us)
Async XLA Ops:
  45.0 13.9 %all-to-all-start.2 = ((f32[4,80,512]{2,1,0:T(8,128)}), f32[4,80,512]{2,1,0:T(8,128)S(1)}, u32[]{:S(2)}, u32[]{:S(2)}) async-start(f32[4,80,512]{2,1,0:T(8,128)} %get-tuple-element.10), calls=%async_computation.2 | async-start | bytes 1310720 | tf_op jit(solution)/shard_map/all_to_all | solution.py:397

commit v5 on v4

--- a/solution.py
+++ b/solution.py
@@ -59,6 +59,7 @@
     phase_hbm,
     scores_ref,
     weighted_ref,
+    share_ref,
     partial_ref,
     images_ref,
     refs_ref,
@@ -122,6 +123,9 @@
     scores_ref[9 * padded + 8 : tables] = group_hot
     group_hot = group_hot.astype(jnp.bfloat16)
     fetches[3].wait()
+    width = share_ref.shape[1]
+    mine = pl.multiple_of(lax.axis_index("dom") * width, width)
+    share_ref[...] = noise_ref[:, pl.ds(mine, width)]
     noise_parts = jnp.concatenate(split_bf16(noise_ref[...]), axis=0)
     weights[...] = lax.dot_general(
         jnp.concatenate([group_hot] * 3, axis=0),
@@ -214,15 +218,11 @@
 
 
 def update_kernel(
-    ngroups, partial_ref, scores_ref, weighted_ref, likelihood_ref, out_hbm, out_ref, sems
+    ngroups, partial_ref, scores_ref, weighted_ref, likelihood_ref, out_ref
 ):
     orients = (out_ref.shape[1] - 8) // 2
     padded = (orients + 7) // 8 * 8
     width = out_ref.shape[2]
-    stores = [
-        pltpu.make_async_copy(out_ref.at[share], out_hbm.at[share], sems.at[share])
-        for share in range(out_ref.shape[0])
-    ]
     likelihood = log_sum(partial_ref[:, 0, :])
     likelihood_ref[...] = likelihood
     rows = 9 * padded + 8
@@ -261,13 +261,10 @@
             there = slice(step * LANES, (step + 1) * LANES)
             out_ref[share, 0:orients, there] = real[0:orients]
             out_ref[share, orients : 2 * orients, there] = imag[0:orients]
-        stores[share].start()
-    for store in stores:
-        store.wait()
-
-
-def divide_kernel(share_ref, received_ref, noise_ref, out_ref):
-    del share_ref
+
+
+def divide_kernel(received_ref, noise_ref, likelihood_ref, out_ref, likelihood_out):
+    likelihood_out[...] = likelihood_ref[...].reshape(likelihood_out.shape)
     rows = received_ref.shape[1]
     width = received_ref.shape[2]
     orients = (rows - 8) // 2
@@ -306,7 +303,7 @@
     return pltpu.CompilerParams(vmem_limit_bytes=limit)
 
 
-def score_call(images, references, noise_weights, log_prior, groups, prior_index, class_map, phase, spread):
+def score_call(images, references, noise_weights, log_prior, groups, prior_index, class_map, phase, spread, shares):
     particles, _, coeffs = images.shape
     orients = references.shape[0]
     padded = (orients + 7) // 8 * 8
@@ -325,10 +322,11 @@
     return pl.pallas_call(
         score_kernel,
         in_specs=[pl.BlockSpec(memory_space=pltpu.HBM)] * 8,
-        out_specs=[pl.BlockSpec(memory_space=pltpu.VMEM)] * 3,
+        out_specs=[pl.BlockSpec(memory_space=pltpu.VMEM)] * 4,
         out_shape=[
             pltpu.VMEM((rows + ngroups + 8 * coeffs // LANES, particles), jnp.float32),
             pltpu.VMEM((particles, 2 * coeffs), jnp.bfloat16),
+            pltpu.VMEM((ngroups, coeffs // shares), jnp.float32),
             jax.ShapeDtypeStruct((spread, 1, particles), jnp.float32),
         ],
         scratch_shapes=[pltpu.VMEM(array.shape, array.dtype) for array in operands]
@@ -357,40 +355,34 @@
     return pl.pallas_call(
         functools.partial(update_kernel, ngroups),
         in_specs=[whole] * 3,
-        out_specs=[whole, pl.BlockSpec(memory_space=pltpu.HBM)],
+        out_specs=[whole] * 2,
         out_shape=[
-            jax.ShapeDtypeStruct((1, particles), jnp.float32),
-            pltpu.HBM(block, jnp.float32),
+            pltpu.VMEM((1, particles), jnp.float32),
+            pltpu.VMEM(block, jnp.float32),
         ],
-        scratch_shapes=[pltpu.VMEM(block, jnp.float32), pltpu.SemaphoreType.DMA((shares,))],
         compiler_params=kernel_params(OTHER_VMEM),
         name="update",
     )(partials, *kept)
 
 
-def divide_call(share, received, noise_weights):
+def divide_call(received, noise_share, likelihood):
     shares, rows, width = received.shape
     orients = (rows - 8) // 2
-    ngroups = noise_weights.shape[0]
+    operands = [
+        pltpu.with_memory_space_constraint(array, pltpu.VMEM)
+        for array in (received, noise_share, likelihood)
+    ]
     return pl.pallas_call(
         divide_kernel,
-        grid_spec=pltpu.PrefetchScalarGridSpec(
-            num_scalar_prefetch=1,
-            grid=(1,),
-            in_specs=[
-                pl.BlockSpec((shares, rows, width), lambda i, s: (0, 0, 0)),
-                pl.BlockSpec((ngroups, width), lambda i, s: (0, s[0])),
-            ],
-            out_specs=pl.BlockSpec((orients * 2 * width // LANES, LANES), lambda i, s: (0, 0)),
-        ),
-        out_shape=jax.ShapeDtypeStruct((orients * 2 * width // LANES, LANES), jnp.float32),
+        in_specs=[pl.BlockSpec(memory_space=pltpu.VMEM)] * 3,
+        out_specs=[pl.BlockSpec(memory_space=pltpu.VMEM)] * 2,
+        out_shape=[
+            jax.ShapeDtypeStruct((orients * 2 * width // LANES, LANES), jnp.float32),
+            jax.ShapeDtypeStruct(likelihood.shape[1:], jnp.float32),
+        ],
         compiler_params=kernel_params(OTHER_VMEM),
         name="divide",
-    )(
-        share,
-        pltpu.with_memory_space_constraint(received, pltpu.VMEM),
-        pltpu.with_memory_space_constraint(noise_weights, pltpu.HBM),
-    )
+    )(*operands)
 
 
 def exchange(spread, axes):
@@ -404,8 +396,8 @@
     depth = lax.axis_size("z")
     plane = lax.axis_size("x") * lax.axis_size("core")
     shares = lax.axis_size("dom")
-    scores, weighted, partial = score_call(
-        images, references, noise_weights, log_prior, groups, prior_index, class_map, phase, plane
+    scores, weighted, noise_share, partial = score_call(
+        images, references, noise_weights, log_prior, groups, prior_index, class_map, phase, plane, shares
     )
     partial = log_sum(exchange(partial, ("x", "core"))[:, 0, :])
     partial = jnp.broadcast_to(partial[None], (depth, 1, partial.shape[1]))
@@ -414,15 +406,14 @@
         partials, scores, weighted, noise_weights.shape[0], orients, shares
     )
     received = exchange(blocks, "dom")
-    share = lax.axis_index("dom").astype(jnp.int32)[None]
-    new_rows = divide_call(share, received, noise_weights)
+    new_rows, likelihood = divide_call(received, noise_share, likelihood)
     width = coeffs // shares
     new_references = (
         new_rows.reshape(orients, width // LANES, 2, LANES)
         .transpose(0, 2, 1, 3)
         .reshape(orients, 2, width)
     )
-    return (new_references, likelihood[0])
+    return (new_references, likelihood)
 
 
 def solution(mesh):

time: 61.1 us -> 59.2 us (0.969)
  the two profiles are of different devices: /device:TPU:2 before, /device:TPU:1 now
where the time goes in v5:
time: 59.2 us; the launch traced here: 58.1 us
  blocking collectives  48.9 us (83%)
  Pallas kernels  8.49 us (14%)
  between operations  0.67 us (1%)
    all_to_all x3, blocking collectives, exchange(): return lax.all_to_all(spread, axes, 0, 0, tiled=True)  48.9 us
    pallas_call x1, Pallas kernels, score_call(): pl.pallas_call(score_kernel, in_specs=[pl.BlockSpec(memory_space=pltpu.HB...  5.62 us
    pallas_call x1, Pallas kernels, update_call(): pl.pallas_call(functools.partial(update_kernel, ngroups), in_specs=[whole...  1.9 us

profile of v5, /device:TPU:1, one launch (start us, length us, event | category | flops | bytes accessed | tf_op | source)
XLA Modules:
  0.0 58.1 jit_solution(7279556640591568340)
XLA Ops:
  0.6 5.6 %score.1 = (f32[560,288]{1,0:T(8,128)S(1)}, bf16[288,4096]{1,0:T(8,128)(2,1)S(1)}, f32[64,512]{1,0:T(8,128)S(1)}, f32[8,1,288]{2,1,0:T(1,128)S(1)}) custom-call(bf16[9216,128]{1,0:T(8,128)(2,1)} %bitcast.21, bf16[1152,128]{1,0:T(8,128)(2,1)} %bitcast.22, f32[64,2048]{1,0:T(8,128)} %noise_hbm.1, f32[8,16]{1,0:T(8,128)} %prior_hbm.1, s32[288]{0:T(512)} %groups_hbm.1, ...), custom_call_target="tpu_custom_call" | custom-call | tf_op jit(solution)/shard_map/score/pallas_call | solution.py:322
  6.3 13.9 %all_to_all.15 = f32[8,1,288]{2,1,0:T(1,128)S(1)} all-to-all(f32[8,1,288]{2,1,0:T(1,128)S(1)} %get-tuple-element.10), channel_id=1, replica_groups=mesh['z'=16,'x'=4,'core'=2,'dom'=4] {'x','core'}, dimensions={0} | all-to-all | bytes 18432 | tf_op jit(solution)/shard_map/all_to_all | solution.py:389
  20.2 22.5 %all_to_all.16.partial_ref = f32[16,1,288]{2,1,0:T(1,128)S(1)} all-to-all(f32[16,1,288]{2,1,0:T(1,128)S(1)} %broadcast_in_dim.2), channel_id=1, replica_groups=mesh['z'=16,'x'=4,'core'=2,'dom'=4] {'z'}, dimensions={0} | all-to-all | bytes 36864 | tf_op jit(solution)/shard_map/all_to_all | solution.py:389
  42.7 1.9 %update.1 = (f32[1,288]{1,0:T(1,128)S(1)}, f32[4,80,512]{2,1,0:T(8,128)S(1)}) custom-call(f32[16,1,288]{2,1,0:T(1,128)S(1)} %all_to_all.16.partial_ref, f32[560,288]{1,0:T(8,128)S(1)} %get-tuple-element.11.scores_ref, bf16[288,4096]{1,0:T(8,128)(2,1)S(1)} %get-tuple-element.12.weighted_ref), custom_call_target="tpu_custom_call" | custom-call | tf_op jit(solution)/shard_map/update/pallas_call | solution.py:355
  44.6 12.5 %all_to_all.17.received_ref = f32[4,80,512]{2,1,0:T(8,128)S(1)} all-to-all(f32[4,80,512]{2,1,0:T(8,128)S(1)} %get-tuple-element.13), channel_id=1, replica_groups=mesh['z'=16,'x'=4,'core'=2,'dom'=4] {'dom'}, dimensions={0} | all-to-all | bytes 1310720 | tf_op jit(solution)/shard_map/all_to_all | solution.py:389
  57.1 1.0 %divide.1 = (f32[288,128]{1,0:T(8,128)}, f32[288]{0:T(512)}) custom-call(f32[4,80,512]{2,1,0:T(8,128)S(1)} %all_to_all.17.received_ref, f32[64,512]{1,0:T(8,128)S(1)} %get-tuple-element.14.noise_ref, f32[1,288]{1,0:T(1,128)S(1)} %get-tuple-element.15.likelihood_ref), custom_call_target="tpu_custom_call" | custom-call | tf_op jit(solution)/shard_map/divide/pallas_call | solution.py:375
  (4 shorter events, 0.1 us)

commit v6 on v5

--- a/solution.py
+++ b/solution.py
@@ -190,10 +190,10 @@
     )
     fetches[7].wait()
 
-    @pl.loop(0, particles // 32)
+    @pl.loop(0, particles // 144)
     def _(g):
-        for h in range(4):
-            spread(images_ref, image_wide, g * 32 + h * 8, 8)
+        for h in range(18):
+            spread(images_ref, image_wide, g * 144 + h * 8, 8)
 
     total = None
     for b in range(blocks):

time: 59.2 us -> 59.2 us (level)
  no operation moved by 1% of the time
where the time goes in v6:
time: 59.2 us; the launch traced here: 58.1 us
  blocking collectives  48.9 us (83%)
  Pallas kernels  8.45 us (14%)
  between operations  0.67 us (1%)
    all_to_all x3, blocking collectives, exchange(): return lax.all_to_all(spread, axes, 0, 0, tiled=True)  48.9 us
    pallas_call x1, Pallas kernels, score_call(): pl.pallas_call(score_kernel, in_specs=[pl.BlockSpec(memory_space=pltpu.HB...  5.59 us
    pallas_call x1, Pallas kernels, update_call(): pl.pallas_call(functools.partial(update_kernel, ngroups), in_specs=[whole...  1.9 us

profile of v6, /device:TPU:1, one launch (start us, length us, event | category | flops | bytes accessed | tf_op | source)
XLA Modules:
  0.0 58.1 jit_solution(11486166497211021391)
XLA Ops:
  0.6 5.6 %score.1 = (f32[560,288]{1,0:T(8,128)S(1)}, bf16[288,4096]{1,0:T(8,128)(2,1)S(1)}, f32[64,512]{1,0:T(8,128)S(1)}, f32[8,1,288]{2,1,0:T(1,128)S(1)}) custom-call(bf16[9216,128]{1,0:T(8,128)(2,1)} %bitcast.21, bf16[1152,128]{1,0:T(8,128)(2,1)} %bitcast.22, f32[64,2048]{1,0:T(8,128)} %noise_hbm.1, f32[8,16]{1,0:T(8,128)} %prior_hbm.1, s32[288]{0:T(512)} %groups_hbm.1, ...), custom_call_target="tpu_custom_call" | custom-call | tf_op jit(solution)/shard_map/score/pallas_call | solution.py:322
  6.2 13.9 %all_to_all.15 = f32[8,1,288]{2,1,0:T(1,128)S(1)} all-to-all(f32[8,1,288]{2,1,0:T(1,128)S(1)} %get-tuple-element.10), channel_id=1, replica_groups=mesh['z'=16,'x'=4,'core'=2,'dom'=4] {'x','core'}, dimensions={0} | all-to-all | bytes 18432 | tf_op jit(solution)/shard_map/all_to_all | solution.py:389
  20.2 22.5 %all_to_all.16.partial_ref = f32[16,1,288]{2,1,0:T(1,128)S(1)} all-to-all(f32[16,1,288]{2,1,0:T(1,128)S(1)} %broadcast_in_dim.2), channel_id=1, replica_groups=mesh['z'=16,'x'=4,'core'=2,'dom'=4] {'z'}, dimensions={0} | all-to-all | bytes 36864 | tf_op jit(solution)/shard_map/all_to_all | solution.py:389
  42.7 1.9 %update.1 = (f32[1,288]{1,0:T(1,128)S(1)}, f32[4,80,512]{2,1,0:T(8,128)S(1)}) custom-call(f32[16,1,288]{2,1,0:T(1,128)S(1)} %all_to_all.16.partial_ref, f32[560,288]{1,0:T(8,128)S(1)} %get-tuple-element.11.scores_ref, bf16[288,4096]{1,0:T(8,128)(2,1)S(1)} %get-tuple-element.12.weighted_ref), custom_call_target="tpu_custom_call" | custom-call | tf_op jit(solution)/shard_map/update/pallas_call | solution.py:355
  44.6 12.5 %all_to_all.17.received_ref = f32[4,80,512]{2,1,0:T(8,128)S(1)} all-to-all(f32[4,80,512]{2,1,0:T(8,128)S(1)} %get-tuple-element.13), channel_id=1, replica_groups=mesh['z'=16,'x'=4,'core'=2,'dom'=4] {'dom'}, dimensions={0} | all-to-all | bytes 1310720 | tf_op jit(solution)/shard_map/all_to_all | solution.py:389
  57.1 1.0 %divide.1 = (f32[288,128]{1,0:T(8,128)}, f32[288]{0:T(512)}) custom-call(f32[4,80,512]{2,1,0:T(8,128)S(1)} %all_to_all.17.received_ref, f32[64,512]{1,0:T(8,128)S(1)} %get-tuple-element.14.noise_ref, f32[1,288]{1,0:T(1,128)S(1)} %get-tuple-element.15.likelihood_ref), custom_call_target="tpu_custom_call" | custom-call | tf_op jit(solution)/shard_map/divide/pallas_call | solution.py:375
  (4 shorter events, 0.1 us)
